TPU v7x, 32 devices: a whole 2x2x4 slice. The times are simulated.
32 devices in a mesh: ctx: 8 (over y, x, core), head: 4 (over z).
Axes of the slice: x: 2, y: 2, z: 4, core: 2. Of those that a mesh axis runs over, the one named last changes fastest.
Arguments:
- queries: bfloat16 [4096, 2048], P('ctx', 'head'), may hold values from -6 to 6
- keys: bfloat16 [4096, 2048], P('ctx', 'head'), may hold values from -0.59765625 to 0.59765625
- values: bfloat16 [4096, 2048], P('ctx', 'head'), may hold values from -6 to 6
- log_decay: float32 [4096, 16], P('ctx', 'head'), may hold values from -0.76 to 0, as said below
- gain: float32 [2048], P('head'), may hold values from 0.1 to 1.9
- upstream: bfloat16 [4096, 2048], P('ctx', 'head'), may hold values from -6 to 6
Outputs:
- grad_queries: bfloat16 [4096, 2048], P('ctx', 'head')
- grad_keys: bfloat16 [4096, 2048], P('ctx', 'head')
- grad_values: bfloat16 [4096, 2048], P('ctx', 'head')
Inputs may be any that keep to these rules, and one draw needn't show every extreme that they name: `log_decay`: the logarithm of the decay that each head applies at each token.
All inputs are finite; a program needn't handle non-finite values.
Results may differ from a plain program's by a relative error of at most 0.0054.
Values sent between devices are 32-bit elements; how exact they have to be, the bound alone decides.
A program may use at most 64 MiB of HBM per device.

v0:
```python
import jax
import jax.numpy as jnp
from jax import lax
from jax.sharding import PartitionSpec as P

BLK = 512


HIGHEST = lax.Precision.HIGHEST
EPSILON = 1e-06


def decay_matrix(cumulative):
    columns = cumulative.T
    spread = columns[:, :, None] - columns[:, None, :]
    positions = jnp.arange(cumulative.shape[0])
    causal = (positions[:, None] >= positions[None, :])[None]
    return jnp.where(causal, jnp.exp(jnp.where(causal, spread, 0.0)), 0.0)


def slab_weights(levels, own_index, later):
    positions = jnp.arange(levels.shape[0])
    source = positions[:, None]
    central_segment = positions[None, :]
    if later:
        between = (central_segment < source) & (central_segment > own_index)
        wanted = positions > own_index
    else:
        between = (central_segment > source) & (central_segment < own_index)
        wanted = positions < own_index
    span_sums = jnp.dot(between.astype(jnp.float32), levels, precision=HIGHEST)
    return jnp.where(wanted[:, None], jnp.exp(span_sums), 0.0)


def fold_blocks(running, segment_members):
    level_sum, summary = running
    block_total, block_state = segment_members
    return (
        (level_sum + block_total, jnp.exp(block_total)[:, None, None] * summary + block_state),
        None,
    )


def on_device(queries, keys, values, log_decay, gain, upstream):
    token_count = queries.shape[0]
    head_count = log_decay.shape[1]
    width_per_head = queries.shape[1] // head_count
    full_width = queries.shape[1] * lax.axis_size("head")
    block_count = token_count // BLK
    block_shape = (block_count, BLK, head_count, width_per_head)
    query_blocks = queries.reshape(block_shape)
    key_blocks = keys.reshape(block_shape)
    value_blocks = values.reshape(block_shape)
    cumulative = jnp.cumsum(log_decay.reshape(block_count, BLK, head_count), axis=1)
    totals = cumulative[:, -1, :]
    ending = jnp.exp(totals[:, None, :] - cumulative)
    weighted_keys = (key_blocks.astype(jnp.float32) * ending[..., None]).astype(jnp.bfloat16)
    block_states = jnp.einsum(
        "nbhe,nbhf->nhef", weighted_keys, value_blocks, preferred_element_type=jnp.float32
    )
    blank_level_start = jnp.zeros((head_count,), jnp.float32)
    empty_state = jnp.zeros((head_count, width_per_head, width_per_head), jnp.float32)
    (slab_level, slab_state), _ = lax.scan(
        fold_blocks, (blank_level_start, empty_state), (totals, block_states)
    )
    own_index = lax.axis_index("ctx")
    levels, states = (
        lax.all_gather(slab_level[None], "ctx", axis=0, tiled=True),
        lax.all_gather(slab_state[None], "ctx", axis=0, tiled=True),
    )
    weights = slab_weights(levels, own_index, False)
    start_state = jnp.einsum("nh,nhef->hef", weights, states, precision=HIGHEST)

    def forward_block(carried_over_state, segment_members):
        query_block, key_block, value_block, cum_block, total_block, state_block = segment_members
        decays = decay_matrix(cum_block)
        carried = (
            jnp.einsum(
                "the,hef->thf",
                query_block.astype(jnp.float32),
                carried_over_state,
                precision=HIGHEST,
            )
            * jnp.exp(cum_block)[:, :, None]
        )
        scores = jnp.einsum(
            "the,she->hts", query_block, key_block, preferred_element_type=jnp.float32
        )
        mixing = (scores * decays).astype(jnp.bfloat16)
        attended = carried + jnp.einsum(
            "hts,shf->thf", mixing, value_block, preferred_element_type=jnp.float32
        )
        new_state = jnp.exp(total_block)[:, None, None] * carried_over_state + state_block
        return (new_state, (attended, carried_over_state))

    _, (attended_all, opening_indices) = lax.scan(
        forward_block,
        start_state,
        (query_blocks, key_blocks, value_blocks, cumulative, totals, block_states),
    )
    attended = attended_all.reshape(token_count, -1)
    scaled_grad = gain * upstream.astype(jnp.float32)
    square_sum, mutual_accumulation = lax.psum(
        (jnp.sum(attended * attended, axis=1), jnp.sum(scaled_grad * attended, axis=1)), "head"
    )
    inverse = lax.rsqrt(square_sum / full_width + EPSILON)
    grad_out = (
        inverse[:, None] * scaled_grad
        - attended * (inverse * inverse * inverse * mutual_accumulation / full_width)[:, None]
    ).astype(jnp.bfloat16)
    grad_blocks = grad_out.reshape(block_shape)
    weighted_queries = (query_blocks.astype(jnp.float32) * jnp.exp(cumulative)[..., None]).astype(
        jnp.bfloat16
    )
    block_grads = jnp.einsum(
        "nbhe,nbhf->nhef", weighted_queries, grad_blocks, preferred_element_type=jnp.float32
    )
    (back_level, slab_grad), _ = lax.scan(
        fold_blocks, (blank_level_start, empty_state), (totals, block_grads), reverse=True
    )
    back_levels, back_states = (
        lax.all_gather(back_level[None], "ctx", axis=0, tiled=True),
        lax.all_gather(slab_grad[None], "ctx", axis=0, tiled=True),
    )
    back_weights = slab_weights(back_levels, own_index, True)
    end_state = jnp.einsum("nh,nhef->hef", back_weights, back_states, precision=HIGHEST)

    def backward_block(after_state, segment_members):
        (
            query_block,
            key_block,
            value_block,
            grad_block,
            cum_block,
            total_block,
            grad_state,
            start_block,
        ) = segment_members
        decays = decay_matrix(cum_block)
        ending_block = jnp.exp(total_block[None, :] - cum_block)[:, :, None]
        scores = jnp.einsum(
            "the,she->hts", query_block, key_block, preferred_element_type=jnp.float32
        )
        mixing = (scores * decays).astype(jnp.bfloat16)
        grad_scores = jnp.einsum(
            "thf,shf->hts", grad_block, value_block, preferred_element_type=jnp.float32
        )
        grad_mixing = (grad_scores * decays).astype(jnp.bfloat16)
        grad_query = (
            jnp.einsum(
                "thf,hef->the", grad_block.astype(jnp.float32), start_block, precision=HIGHEST
            )
            * jnp.exp(cum_block)[:, :, None]
        )
        grad_query = grad_query + jnp.einsum(
            "hts,she->the", grad_mixing, key_block, preferred_element_type=jnp.float32
        )
        grad_key = (
            jnp.einsum(
                "shf,hef->she", value_block.astype(jnp.float32), after_state, precision=HIGHEST
            )
            * ending_block
        )
        grad_key = grad_key + jnp.einsum(
            "hts,the->she", grad_mixing, query_block, preferred_element_type=jnp.float32
        )
        grad_value = (
            jnp.einsum(
                "she,hef->shf", key_block.astype(jnp.float32), after_state, precision=HIGHEST
            )
            * ending_block
        )
        grad_value = grad_value + jnp.einsum(
            "hts,thf->shf", mixing, grad_block, preferred_element_type=jnp.float32
        )
        before_state = jnp.exp(total_block)[:, None, None] * after_state + grad_state
        return (
            before_state,
            (
                grad_query.astype(jnp.bfloat16),
                grad_key.astype(jnp.bfloat16),
                grad_value.astype(jnp.bfloat16),
            ),
        )

    _, (grad_q_all, grad_k_all, grad_v_all) = lax.scan(
        backward_block,
        end_state,
        (
            query_blocks,
            key_blocks,
            value_blocks,
            grad_blocks,
            cumulative,
            totals,
            block_grads,
            opening_indices,
        ),
        reverse=True,
    )
    return (
        grad_q_all.reshape(token_count, -1),
        grad_k_all.reshape(token_count, -1),
        grad_v_all.reshape(token_count, -1),
    )


def solution(mesh):
    placed = (
        P("ctx", "head"),
        P("ctx", "head"),
        P("ctx", "head"),
        P("ctx", "head"),
        P("head"),
        P("ctx", "head"),
    )
    return jax.shard_map(
        on_device,
        mesh=mesh,
        in_specs=placed,
        out_specs=(P("ctx", "head"), P("ctx", "head"), P("ctx", "head")),
        check_vma=False,
    )
```

profile of v0, /device:TPU:0, one launch (start us, length us, event | category | flops | bytes accessed | tf_op | source)
XLA Modules:
  0.0 106.1 jit_solution(14236776284797388537)
XLA Ops:
  7.2 0.0 copy-start
  7.2 0.0 all-gather.6.cloned.1.call-start
  7.2 0.8 reshape.187
  8.0 1.2 %reduce-window.6 = f32[1,4,4,128]{3,2,1,0:T(4,128)S(1)} reduce-window(f32[1,4,4,128]{3,2,1,0:T(4,128)S(1)} %reshape.187, f32[]{:T(128)} %constant.71.clone.1), window={size=1x1x1x128 pad=0_0x0_0x0_0x127_0}, to_apply=%region_0.0 | reduce-window | flops 260096 | bytes 16388 | tf_op jit(solution)/shard_map/reduce-window
  9.2 0.2 slice_reduce_fusion
  9.4 0.2 reduce-window.9
  9.6 0.1 broadcast.68
  9.7 0.2 slice_reduce_fusion.1
  9.9 0.1 exponential_bitcast_fusion.1
  10.0 0.0 copy-start.9
  10.0 1.3 %copy.197 = bf16[512,512]{0,1:T(8,128)(2,1)S(1)} copy(bf16[512,512]{1,0:T(8,128)(2,1)} %param.7) | data formatting | bytes 1048576 | tf_op jit(solution)/shard_map/reshape | solution.py:52
  11.3 0.0 copy-start.7
  11.3 1.0 convolution_add_fusion.1
  12.3 0.0 all-gather.6.cloned.1.call-update
  12.4 0.0 all-gather.8.cloned.1.call-start
  12.4 0.1 copy.130
  12.5 10.2 %all-gather = f32[8,1,4]{2,1,0:T(1,128)S(1)} all-gather(f32[1,1,4]{2,1,0:T(1,128)S(1)} %copy.130), channel_id=2, replica_groups=mesh['ctx'=8,'head'=4] {'ctx'}, dimensions={0}, use_global_device_ids=true | all-gather | bytes 144 | tf_op jit(solution)/shard_map/all_gather | solution.py:68
  22.7 0.2 copy.165
  22.9 0.1 iota_compare_fusion
  23.0 0.2 fusion.16
  23.2 0.1 fusion.31
  23.3 1.6 %multiply_convert_fusion.1 = bf16[4,512,512]{2,1,0:T(8,128)(2,1)S(1)} fusion(bf16[512,4,128]{0,2,1:T(8,128)(2,1)S(1)} %bitcast.138, f32[4,512]{1,0:T(4,128)S(1)} %bitcast.159, pred[512,512]{1,0:T(8,128)(4,1)S(1)} %iota_compare_fusion, bf16[512,512]{1,0:T(8,128)(2,1)S(1)} %copy-done.9), kind=kOutput, calls=%fused_computation.1 | convolution fusion | flops 273678336 | bytes 3416064 | tf_op jit(solution)/shard_map/while/body/eval_jaxpr/the,she->hts/dot_general | solution.py:86
  24.9 1.3 %copy-done.1 = bf16[4,512,512]{2,1,0:T(8,128)(2,1)} copy-done((bf16[4,512,512]{2,1,0:T(8,128)(2,1)}, bf16[4,512,512]{2,1,0:T(8,128)(2,1)S(1)}, u32[]{:S(2)}) %copy-start.1) | copy-done | bytes 2097176
  26.2 0.8 convolution_bitcast_fusion.3
  27.0 16.1 %all-gather.6.cloned.1.call-done = f32[32,128,128]{2,1,0:T(8,128)} async-done(((f32[4,128,128]{2,1,0:T(8,128)}), f32[32,128,128]{2,1,0:T(8,128)}) %all-gather.6.cloned.1.call-update) | async-done | bytes 2097168 | tf_op jit(solution)/shard_map/all_gather | solution.py:69
  43.1 4.4 %fusion.2 = f32[4,1,128,128]{3,1,2,0:T(1,128)S(1)} fusion(f32[8,4,1,1]{0,2,3,1:T(1,128)S(1)} %bitcast.166, f32[8,4,128,128]{3,2,1,0:T(8,128)} %bitcast.153), kind=kOutput, calls=%fused_computation.5 | convolution fusion | flops 6291456 | bytes 2359424 | tf_op jit(solution)/shard_map/nh,nhef->hef/dot_general | solution.py:72
  47.5 0.0 copy-start.14
  47.5 0.7 multiply_reduce_fusion.1
  48.3 0.3 copy.140
  48.6 1.3 %multiply_reduce_fusion = f32[512]{0:T(512)S(1)} fusion(f32[512,512]{1,0:T(8,128)S(1)} %copy.140, bf16[512,512]{1,0:T(8,128)(2,1)} %param.11, f32[512]{0:T(512)S(1)} %copy-done.14), kind=kLoop, calls=%fused_computation.34 | loop fusion | flops 1048064 | bytes 1576960 | tf_op jit(solution)/shard_map/reduce_sum | solution.py:104
  49.9 11.9 %all-reduce = (f32[512]{0:T(512)S(1)}, f32[512]{0:T(512)S(1)}) all-reduce(f32[512]{0:T(512)S(1)} %multiply_reduce_fusion, f32[512]{0:T(512)S(1)} %get-tuple-element.114), channel_id=1, replica_groups=mesh['ctx'=8,'head'=4] {'head'}, use_global_device_ids=true, to_apply=%region_5.6 | all-reduce | flops 1024 | bytes 8192 | tf_op jit(solution)/shard_map/psum | solution.py:103
  61.8 1.3 %subtract_convert_fusion = bf16[512,512]{1,0:T(8,128)(2,1)S(1)} fusion(f32[512,512]{1,0:T(8,128)S(1)} %copy.140, bf16[512,512]{1,0:T(8,128)(2,1)} %param.11, f32[512]{0:T(512)S(1)} %get-tuple-element.113, f32[512]{0:T(512)S(1)} %copy-done.14, f32[512]{0:T(512)S(1)} %get-tuple-element.112), kind=kLoop, calls=%fused_computation.33 | loop fusion | flops 1572864 | bytes 2103296 | tf_op jit(solution)/shard_map/convert_element_type | solution.py:110
  63.1 0.2 copy.166
  63.3 1.0 convolution_add_fusion
  64.3 0.0 all-gather.8.cloned.1.call-update
  64.3 0.2 fusion.15
  64.5 1.6 %multiply_convert_fusion = bf16[4,512,512]{2,1,0:T(8,128)(2,1)S(1)} fusion(bf16[512,4,128]{0,2,1:T(8,128)(2,1)S(1)} %bitcast.143, f32[4,512]{1,0:T(4,128)S(1)} %bitcast.160, pred[512,512]{1,0:T(8,128)(4,1)S(1)} %copy-done.13, bf16[512,512]{1,0:T(8,128)(2,1)S(1)} %copy-done), kind=kOutput, calls=%fused_computation | convolution fusion | flops 273678336 | bytes 3416064 | tf_op jit(solution)/shard_map/while/body/eval_jaxpr/thf,shf->hts/dot_general | solution.py:145
  66.1 0.8 convolution_bitcast_fusion.2
  66.9 2.6 %fusion.12 = bf16[512,4,128]{0,2,1:T(8,128)(2,1)} fusion(f32[512,4,128]{0,2,1:T(8,128)S(1)} %convolution_bitcast_fusion.2, f32[4,128,128]{2,1,0:T(8,128)S(1)} %bitcast.148, bf16[512,4,128]{0,2,1:T(8,128)(2,1)} %bitcast.144, f32[512,4]{0,1:T(4,128)S(1)} %get-tuple-element.109), kind=kOutput, calls=%fused_computation.23 | convolution fusion | flops 403439616 | bytes 2367488 | tf_op jit(solution)/shard_map/while/body/eval_jaxpr/thf,hef->the/dot_general | solution.py:150
  69.6 2.0 %copy.152 = bf16[512,512]{1,0:T(8,128)(2,1)} copy(bf16[512,512]{0,1:T(8,128)(2,1)} %bitcast.155) | data formatting | bytes 1048576
  71.6 2.6 %convolution_bitcast_fusion.1 = f32[512,4,128]{0,2,1:T(8,128)} fusion(bf16[512,4,128]{0,2,1:T(8,128)(2,1)} %bitcast.145, bf16[4,512,512]{2,1,0:T(8,128)(2,1)S(1)} %copy-done.2), kind=kOutput, calls=%fused_computation.8 | convolution fusion | flops 268435456 | bytes 3670016 | tf_op jit(solution)/shard_map/while/body/eval_jaxpr/hts,thf->shf/dot_general | solution.py:173
  74.2 0.4 convolution_bitcast_fusion
  74.7 14.9 %all-gather.8.cloned.1.call-done = f32[32,128,128]{2,1,0:T(8,128)} async-done(((f32[4,128,128]{2,1,0:T(8,128)}), f32[32,128,128]{2,1,0:T(8,128)}) %all-gather.8.cloned.1.call-update) | async-done | bytes 2097168 | tf_op jit(solution)/shard_map/all_gather | solution.py:123
  89.6 4.5 %fusion = f32[4,1,128,128]{3,1,2,0:T(1,128)S(1)} fusion(f32[8,4,1,1]{0,2,3,1:T(1,128)S(1)} %bitcast.165, f32[8,4,128,128]{3,2,1,0:T(8,128)} %bitcast.154), kind=kOutput, calls=%fused_computation.3 | convolution fusion | flops 6291456 | bytes 2359424 | tf_op jit(solution)/shard_map/nh,nhef->hef/dot_general | solution.py:126
  94.1 1.5 %fusion.14 = bf16[512,4,128]{0,2,1:T(8,128)(2,1)} fusion(f32[512,4,128]{0,2,1:T(8,128)S(1)} %copy-done.6, f32[4,128,128]{2,1,0:T(8,128)S(1)} %bitcast.149, f32[512,4]{0,1:T(4,128)S(1)} %get-tuple-element.108, bf16[512,512]{1,0:T(8,128)(2,1)S(1)} %copy-done.10), kind=kOutput, calls=%fused_computation.25 | convolution fusion | flops 403439616 | bytes 2367488 | tf_op jit(solution)/shard_map/while/body/eval_jaxpr/she,hef->shf/dot_general | solution.py:168
  95.6 2.0 %copy.154 = bf16[512,512]{1,0:T(8,128)(2,1)} copy(bf16[512,512]{0,1:T(8,128)(2,1)} %bitcast.157) | data formatting | bytes 1048576
  97.6 0.6 fusion.13
  98.2 1.0 copy.153
  (32 shorter events, 0.1 us)
Async XLA Ops:
  7.2 4.2 %copy-start = (bf16[512,512]{1,0:T(8,128)(2,1)S(1)}, bf16[512,512]{1,0:T(8,128)(2,1)}, u32[]{:S(2)}) copy-start(bf16[512,512]{1,0:T(8,128)(2,1)} %param.8) | copy-start | bytes 1572868
  7.2 15.5 %copy-start.11 = (bf16[512,512]{1,0:T(8,128)(2,1)S(1)}, bf16[512,512]{1,0:T(8,128)(2,1)}, u32[]{:S(2)}) copy-start(bf16[512,512]{1,0:T(8,128)(2,1)} %param.6) | copy-start | bytes 1572868
  7.2 35.9 %all-gather.6.cloned.1.call-start = ((), (), s32[]{:S(2)}) async-start(), calls=%async_computation | async-start | bytes 2359296 | tf_op jit(solution)/shard_map/all_gather | solution.py:69
  10.0 13.3 %copy-start.9 = (bf16[512,512]{1,0:T(8,128)(2,1)S(1)}, bf16[512,512]{1,0:T(8,128)(2,1)}, u32[]{:S(2)}) copy-start(bf16[512,512]{1,0:T(8,128)(2,1)} %param.7) | copy-start | bytes 1572868
  11.3 11.4 %copy-start.7 = (bf16[512,512]{0,1:T(8,128)(2,1)}, bf16[512,512]{0,1:T(8,128)(2,1)S(1)}, u32[]{:S(2)}) copy-start(bf16[512,512]{0,1:T(8,128)(2,1)S(1)} %copy.197) | copy-start | bytes 1572868
  12.4 77.3 %all-gather.8.cloned.1.call-start = ((), (), s32[]{:S(2)}) async-start(), calls=%async_computation.1 | async-start | bytes 2359296 | tf_op jit(solution)/shard_map/all_gather | solution.py:123
  23.0 1.8 %copy-start.12 = (pred[512,512]{1,0:T(8,128)(4,1)}, pred[512,512]{1,0:T(8,128)(4,1)S(1)}, u32[]{:S(2)}) copy-start(pred[512,512]{1,0:T(8,128)(4,1)S(1)} %iota_compare_fusion) | copy-start | bytes 786436
  24.9 1.3 %copy-start.1 = (bf16[4,512,512]{2,1,0:T(8,128)(2,1)}, bf16[4,512,512]{2,1,0:T(8,128)(2,1)S(1)}, u32[]{:S(2)}) copy-start(bf16[4,512,512]{2,1,0:T(8,128)(2,1)S(1)} %multiply_convert_fusion.1) | copy-start | bytes 6291460
  47.5 1.1 %copy-start.14 = (f32[512]{0:T(512)S(1)}, f32[512]{0:T(512)}, u32[]{:S(2)}) copy-start(f32[512]{0:T(512)} %param.10) | copy-start | bytes 6148
  61.8 2.8 %copy-start.13 = (pred[512,512]{1,0:T(8,128)(4,1)S(1)}, pred[512,512]{1,0:T(8,128)(4,1)}, u32[]{:S(2)}) copy-start(pred[512,512]{1,0:T(8,128)(4,1)} %copy-done.12) | copy-start | bytes 786436
  63.3 2.8 %copy-start.5 = (bf16[512,512]{0,1:T(8,128)(2,1)}, bf16[512,512]{0,1:T(8,128)(2,1)S(1)}, u32[]{:S(2)}) copy-start(bf16[512,512]{0,1:T(8,128)(2,1)S(1)} %copy.166) | copy-start | bytes 1572868
  64.5 1.6 %copy-start.8 = (bf16[512,512]{0,1:T(8,128)(2,1)S(1)}, bf16[512,512]{0,1:T(8,128)(2,1)}, u32[]{:S(2)}) copy-start(bf16[512,512]{0,1:T(8,128)(2,1)} %copy-done.7) | copy-start | bytes 1572868
  66.1 3.4 %copy-start.3 = (bf16[4,512,512]{2,1,0:T(8,128)(2,1)}, bf16[4,512,512]{2,1,0:T(8,128)(2,1)S(1)}, u32[]{:S(2)}) copy-start(bf16[4,512,512]{2,1,0:T(8,128)(2,1)S(1)} %multiply_convert_fusion) | copy-start | bytes 6291460
  66.9 4.7 %copy-start.2 = (bf16[4,512,512]{2,1,0:T(8,128)(2,1)S(1)}, bf16[4,512,512]{2,1,0:T(8,128)(2,1)}, u32[]{:S(2)}) copy-start(bf16[4,512,512]{2,1,0:T(8,128)(2,1)} %copy-done.1) | copy-start | bytes 6291460
  71.6 2.6 %copy-start.4 = (bf16[4,512,512]{2,1,0:T(8,128)(2,1)S(1)}, bf16[4,512,512]{2,1,0:T(8,128)(2,1)}, u32[]{:S(2)}) copy-start(bf16[4,512,512]{2,1,0:T(8,128)(2,1)} %copy-done.3) | copy-start | bytes 6291460
  74.7 19.4 %copy-start.6 = (f32[512,4,128]{0,2,1:T(8,128)S(1)}, f32[512,4,128]{0,2,1:T(8,128)}, u32[]{:S(2)}) copy-start(f32[512,4,128]{0,2,1:T(8,128)} %convolution_bitcast_fusion.1) | copy-start | bytes 3145732
  89.6 4.5 %copy-start.10 = (bf16[512,512]{1,0:T(8,128)(2,1)S(1)}, bf16[512,512]{1,0:T(8,128)(2,1)}, u32[]{:S(2)}) copy-start(bf16[512,512]{1,0:T(8,128)(2,1)} %param.7) | copy-start | bytes 1572868
Sparse Core Ops, SparseCore 0:
  12.5 30.5 all-gather.5
  64.5 25.1 all-gather.7
where the time goes:
time: 107 us; the launch traced here: 106 us
  waiting for transfers between devices  31.1 us (29%)
  matrix products  24.4 us (23%)
  blocking collectives  22.1 us (21%)
  between operations  14.3 us (13%)
  local copies, waits for them, and re-layouts  9.88 us (9%)
  other arithmetic  4.23 us (4%)
    all_gather x1, waiting for transfers between devices, on_device(): lax.all_gather(slab_state[None], 'ctx', axis=0, tiled=True)  16.1 us
    all_gather x1, waiting for transfers between devices, on_device(): lax.all_gather(slab_grad[None], 'ctx', axis=0, tiled=True)  14.9 us
    psum x1, blocking collectives, on_device(): lax.psum((jnp.sum(attended * attended, axis=1), jnp.sum(scaled_grad * att...  11.9 us
    all_gather x1, blocking collectives, on_device(): lax.all_gather(slab_level[None], 'ctx', axis=0, tiled=True)  10.2 us
    unnamed x33, local copies, waits for them, and re-layouts  6.47 us
    dot_general x1, matrix products, on_device(): jnp.einsum('nh,nhef->hef', back_weights, back_states, precision=HIGHEST)  4.48 us
    dot_general x1, matrix products, on_device(): start_state = jnp.einsum('nh,nhef->hef', weights, states, precision=HIGHEST)  4.42 us
    dot_general x1, matrix products, backward_block(): jnp.einsum('hts,thf->shf', mixing, grad_block, preferred_element_type=jnp...  2.62 us
  transfers between devices with their start and end apart: 2, of which 2 were waited for; matrix products, arithmetic and copies ran while one was open for 13% of the time, Pallas kernels for 0%

commit v1 on v0

v1 whole, which is shorter than its diff:
```python
import functools

import jax
import jax.numpy as jnp
from jax import lax
from jax.experimental import pallas as pl
from jax.experimental.pallas import tpu as pltpu
from jax.sharding import PartitionSpec as P

DIM = 128
TILE = 256
EPSILON = 1e-06
MESH = pl.DeviceIdType.MESH
F32 = jnp.float32
BF16 = jnp.bfloat16


def dot(a, b, dims):
    return lax.dot_general(a, b, ((dims[:1], dims[1:]), ((), ())), preferred_element_type=F32)


def split(x):
    high = x.astype(BF16)
    return high, (x - high.astype(F32)).astype(BF16)


def kernel(
    ctx_n, head_n, width,
    q_hbm, k_hbm, v_hbm, ld_hbm, gain_hbm, up_hbm,
    dq_out, dk_out, dv_out,
    q, k, v, ld, gain, up,
    mix, dec, att, grad, wq, cum, cum_rows, dkp, dvp, dq, dk, dv,
    f_send, f_recv, f_tsend, f_trecv, f_pre,
    b_send, b_recv, b_tsend, b_trecv, b_pre,
    z_send, z_recv,
    in_sem, out_sem,
    fs_sem, fr_sem, fts_sem, ftr_sem, fps_sem, fpr_sem,
    bs_sem, br_sem, bts_sem, btr_sem, bps_sem, bpr_sem,
    zs_sem, zr_sem,
):
    tokens = q.shape[0]
    heads = q.shape[1] // DIM
    half = heads // 2
    bits = ctx_n.bit_length() - 1
    tiles = tokens // TILE
    me = lax.axis_index("ctx")
    zed = lax.axis_index("head")
    core = lax.rem(me, 2)
    own = core * half
    bit_values = [lax.rem(me // (2**b), 2) for b in range(bits)]
    partners = [me + (2**b) * (1 - 2 * bit_values[b]) for b in range(bits)]

    loads = []
    for i, (src, dst) in enumerate(
        ((ld_hbm, ld), (k_hbm, k), (v_hbm, v), (q_hbm, q), (gain_hbm, gain), (up_hbm, up))
    ):
        load = pltpu.make_async_copy(src, dst, in_sem.at[i])
        load.start()
        loads.append(load)
    load_ld, load_k, load_v, load_q, load_gain, load_up = loads

    barrier = pltpu.get_barrier_semaphore()
    for b in range(bits):
        pl.semaphore_signal(barrier, inc=1, device_id=(partners[b], zed), device_id_type=MESH)
    for d in range(1, head_n):
        pl.semaphore_signal(
            barrier, inc=1, device_id=(me, lax.rem(zed + d, head_n)), device_id_type=MESH
        )

    load_ld.wait()
    steps = jnp.pad(ld[...], ((0, 0), (0, DIM - heads)))
    row_id = lax.broadcasted_iota(jnp.int32, (tokens, tokens), 0)
    col_id = lax.broadcasted_iota(jnp.int32, (tokens, tokens), 1)
    lower = jnp.where(row_id >= col_id, 1.0, 0.0).astype(BF16)
    top, rest = split(steps)
    low = (steps - top.astype(F32) - rest.astype(F32)).astype(BF16)
    total_cum = dot(lower, top, (1, 0)) + (dot(lower, rest, (1, 0)) + dot(lower, low, (1, 0)))
    cum[...] = total_cum
    cum_rows[...] = total_cum.T[:8]

    def columns(h):
        return slice(h * DIM, (h + 1) * DIM)

    def cum_column(h):
        return cum[:, h : h + 1]

    def total(h):
        return cum[tokens - 1 : tokens, h : h + 1]

    def level_rows(h):
        return jnp.broadcast_to(total(h), (8, DIM))

    diagonal = lax.broadcasted_iota(jnp.int32, (TILE, TILE), 0) >= lax.broadcasted_iota(
        jnp.int32, (TILE, TILE), 1
    )

    def exchange(rev, send, recv, tsend, trecv, pre, ss, rs, tss, trs, pss, prs):
        pending = []
        state = {}

        def remote(src, dst, s_sem, r_sem, b):
            copy = pltpu.make_async_remote_copy(
                src_ref=src, dst_ref=dst, send_sem=s_sem, recv_sem=r_sem,
                device_id=(partners[b], zed), device_id_type=MESH,
            )
            copy.start()
            pending.append(copy)
            return copy

        def upper(b):
            return (1 - bit_values[b]) if rev else bit_values[b]

        first = []

        def post(h, value):
            send[h, :DIM] = value
            send[h, DIM:] = level_rows(h)
            first.append(remote(send.at[h], recv.at[h], ss.at[h], rs.at[h], 0))

        def pair():
            for copy in first:
                copy.wait_recv()
            is_upper = upper(0) == 1
            for i in range(half):
                o = own + i
                mine, other = send[o, :DIM], recv[o, :DIM]
                my_level, other_level = send[o, DIM : DIM + 1], recv[o, DIM : DIM + 1]
                value = mine * jnp.where(is_upper, 1.0, jnp.exp(other_level)) + other * jnp.where(
                    is_upper, jnp.exp(my_level), 1.0
                )
                state[i] = (value, my_level + other_level, None, None)
                publish(1, i)

        copies = {}

        def publish(b, i):
            value, level, _, _ = state[i]
            slot = (b - 1) * half + i
            tsend[slot, :DIM] = value
            tsend[slot, DIM:] = jnp.broadcast_to(level, (8, DIM))
            copies[b, i] = remote(tsend.at[slot], trecv.at[slot], tss.at[slot], trs.at[slot], b)

        def combine(b):
            is_upper = upper(b) == 1
            for i in range(half):
                copies[b, i].wait_recv()
                slot = (b - 1) * half + i
                _, level, _, before_level = state[i]
                value = tsend[slot, :DIM]
                other, other_level = trecv[slot, :DIM], trecv[slot, DIM : DIM + 1]
                if before_level is None:
                    before = jnp.where(is_upper, other, 0.0)
                    before_level = jnp.where(is_upper, other_level, 0.0)
                else:
                    before = pre[own + i] + jnp.where(is_upper, jnp.exp(before_level), 0.0) * other
                    before_level = before_level + jnp.where(is_upper, other_level, 0.0)
                pre[own + i] = before
                if b + 1 < bits:
                    value = value * jnp.where(is_upper, 1.0, jnp.exp(other_level)) + (
                        other * jnp.where(is_upper, jnp.exp(level), 1.0)
                    )
                    state[i] = (value, level + other_level, None, before_level)
                    publish(b + 1, i)
                else:
                    copies["pre", i] = remote(
                        pre.at[own + i], pre.at[own + i], pss.at[i], prs.at[i], 0
                    )

        def finish():
            for i in range(half):
                copies["pre", i].wait_recv()
            for copy in pending:
                copy.wait_send()

        def result(h):
            outside = pre[h]
            level = recv[h, DIM : DIM + 1]
            return jnp.where(upper(0) == 1, outside * jnp.exp(level) + recv[h, :DIM], outside)

        stages = [pair] + [functools.partial(combine, b) for b in range(1, bits)] + [finish]
        return post, stages, result

    post, stages, start_state = exchange(
        False, f_send, f_recv, f_tsend, f_trecv, f_pre,
        fs_sem, fr_sem, fts_sem, ftr_sem, fps_sem, fpr_sem,
    )

    load_k.wait()
    load_v.wait()
    entered = bits + head_n - 1
    for h in range(heads):
        ending = jnp.exp(total(h) - cum_column(h))
        weighted_keys = (k[:, columns(h)].astype(F32) * ending).astype(BF16)
        value = dot(weighted_keys, v[:, columns(h)], (0, 0))
        if h == 0:
            pl.semaphore_wait(barrier, entered)
        post(h, value)

    load_q.wait()

    def forward(h):
        for i in range(tiles):
            rows = slice(i * TILE, (i + 1) * TILE)
            total_rows = None
            for j in range(i + 1):
                sources = slice(j * TILE, (j + 1) * TILE)
                scores = dot(q[rows, columns(h)], k[sources, columns(h)], (1, 1))
                spread = cum[rows, h : h + 1] - cum_rows[h : h + 1, sources]
                if i == j:
                    spread = jnp.where(diagonal, spread, -1e30)
                decays = jnp.exp(spread)
                dec[h, rows, sources] = decays
                mixing = (scores * decays).astype(BF16)
                mix[h, rows, sources] = mixing
                part = dot(mixing, v[sources, columns(h)], (1, 0))
                total_rows = part if total_rows is None else total_rows + part
            att[rows, columns(h)] = total_rows

    def weigh_queries(h):
        wq[:, columns(h)] = (q[:, columns(h)].astype(F32) * jnp.exp(cum_column(h))).astype(BF16)

    def interleave(works, stages):
        for place in range(max(len(works), len(stages))):
            if place < len(works):
                works[place]()
            if place < len(stages):
                stages[place]()

    interleave([functools.partial(forward, h) for h in range(heads)], stages)

    load_gain.wait()
    load_up.wait()
    squares = None
    for h in range(heads):
        high, low = split(start_state(h))
        queries = q[:, columns(h)]
        carried = dot(
            jnp.concatenate([queries, queries], axis=1), jnp.concatenate([high, low], axis=0), (1, 0)
        )
        value = att[:, columns(h)] + jnp.exp(cum_column(h)) * carried
        att[:, columns(h)] = value
        scaled = gain[:, columns(h)] * up[:, columns(h)].astype(F32)
        square, cross = value * value, scaled * value
        squares = square if squares is None else squares + square
        crosses = cross if h == 0 else crosses + cross
    square_sum = jnp.sum(squares, axis=1, keepdims=True)
    cross_sum = jnp.sum(crosses, axis=1, keepdims=True)
    lane = lax.broadcasted_iota(jnp.int32, (tokens, DIM), 1)
    packed = jnp.where(lane == 0, square_sum, jnp.where(lane == 1, cross_sum, 0.0))
    z_send[...] = packed.T[:8]
    z_copies = []
    for d in range(1, head_n):
        copy = pltpu.make_async_remote_copy(
            src_ref=z_send, dst_ref=z_recv.at[d - 1],
            send_sem=zs_sem.at[d - 1], recv_sem=zr_sem.at[d - 1],
            device_id=(me, lax.rem(zed + d, head_n)), device_id_type=MESH,
        )
        copy.start()
        z_copies.append(copy)
    for h in range(heads):
        weigh_queries(h)
    sums = z_send[...]
    for d in range(1, head_n):
        z_copies[d - 1].wait_recv()
        sums = sums + z_recv[d - 1]
    full = jnp.concatenate([sums, jnp.zeros((DIM - 8, tokens), F32)], axis=0).T
    square_sum, cross_sum = full[:, 0:1], full[:, 1:2]
    inverse = lax.rsqrt(square_sum / width + EPSILON)
    factor = inverse * inverse * inverse * cross_sum / width

    post, stages, end_state = exchange(
        True, b_send, b_recv, b_tsend, b_trecv, b_pre,
        bs_sem, br_sem, bts_sem, btr_sem, bps_sem, bpr_sem,
    )
    for h in range(heads):
        scaled = gain[:, columns(h)] * up[:, columns(h)].astype(F32)
        value = (inverse * scaled - att[:, columns(h)] * factor).astype(BF16)
        grad[:, columns(h)] = value
        post(h, dot(wq[:, columns(h)], value, (0, 0)))
    for copy in z_copies:
        copy.wait_send()

    stores = []

    def store(i, h, src, dst):
        copy = pltpu.make_async_copy(
            src.at[:, columns(h)], dst.at[:, columns(h)], out_sem.at[i * heads + h]
        )
        copy.start()
        stores.append(copy)

    def backward(h):
        high, low = split(start_state(h))
        states = jnp.concatenate([high, low], axis=1)
        key_sums, value_sums = [None] * tiles, [None] * tiles
        for i in range(tiles):
            rows = slice(i * TILE, (i + 1) * TILE)
            grads = grad[rows, columns(h)]
            query_sum = jnp.exp(cum[rows, h : h + 1]) * dot(
                jnp.concatenate([grads, grads], axis=1), states, (1, 1)
            )
            for j in range(i + 1):
                sources = slice(j * TILE, (j + 1) * TILE)
                scores = dot(grads, v[sources, columns(h)], (1, 1))
                mixing = (scores * dec[h, rows, sources]).astype(BF16)
                query_sum = query_sum + dot(mixing, k[sources, columns(h)], (1, 0))
                key_part = dot(mixing, q[rows, columns(h)], (0, 0))
                value_part = dot(mix[h, rows, sources], grads, (0, 0))
                key_sums[j] = key_part if i == j else key_sums[j] + key_part
                value_sums[j] = value_part if i == j else value_sums[j] + value_part
            dq[rows, columns(h)] = query_sum.astype(BF16)
        store(0, h, dq, dq_out)
        for j in range(tiles):
            sources = slice(j * TILE, (j + 1) * TILE)
            dkp[sources, columns(h)] = key_sums[j]
            dvp[sources, columns(h)] = value_sums[j]

    interleave([functools.partial(backward, h) for h in range(heads)], stages)

    for h in range(heads):
        high, low = split(end_state(h))
        ending = jnp.exp(total(h) - cum_column(h))
        keys, values = k[:, columns(h)], v[:, columns(h)]
        key_carried = dot(
            jnp.concatenate([values, values], axis=1), jnp.concatenate([high, low], axis=1), (1, 1)
        )
        dk[:, columns(h)] = (ending * key_carried + dkp[:, columns(h)]).astype(BF16)
        store(1, h, dk, dk_out)
        value_carried = dot(
            jnp.concatenate([keys, keys], axis=1), jnp.concatenate([high, low], axis=0), (1, 0)
        )
        dv[:, columns(h)] = (ending * value_carried + dvp[:, columns(h)]).astype(BF16)
        store(2, h, dv, dv_out)
    for copy in stores:
        copy.wait()


def on_device(queries, keys, values, log_decay, gain, upstream):
    tokens, local = queries.shape
    heads = log_decay.shape[1]
    ctx_n, head_n = lax.axis_size("ctx"), lax.axis_size("head")
    steps = ctx_n.bit_length() - 2
    half = heads // 2
    wide = (tokens, local)
    message = (heads, DIM + 8, DIM)
    chip_message = (steps * half, DIM + 8, DIM)
    states = [
        pltpu.VMEM(message, F32),
        pltpu.VMEM(message, F32),
        pltpu.VMEM(chip_message, F32),
        pltpu.VMEM(chip_message, F32),
        pltpu.VMEM((heads, DIM, DIM), F32),
    ]
    dma = pltpu.SemaphoreType.DMA
    state_sems = [
        dma((heads,)), dma((heads,)), dma((steps * half,)), dma((steps * half,)),
        dma((half,)), dma((half,)),
    ]
    anywhere = pl.BlockSpec(memory_space=pl.ANY)
    out = jax.ShapeDtypeStruct(wide, BF16)
    return pl.pallas_call(
        functools.partial(kernel, ctx_n, head_n, local * head_n),
        out_shape=(out, out, out),
        in_specs=[anywhere] * 6,
        out_specs=(anywhere,) * 3,
        scratch_shapes=[
            pltpu.VMEM(wide, BF16),
            pltpu.VMEM(wide, BF16),
            pltpu.VMEM(wide, BF16),
            pltpu.VMEM(log_decay.shape, F32),
            pltpu.VMEM((1, local), F32),
            pltpu.VMEM(wide, BF16),
            pltpu.VMEM((heads, tokens, tokens), BF16),
            pltpu.VMEM((heads, tokens, tokens), F32),
            pltpu.VMEM(wide, F32),
            pltpu.VMEM(wide, BF16),
            pltpu.VMEM(wide, BF16),
            pltpu.VMEM((tokens, DIM), F32),
            pltpu.VMEM((8, tokens), F32),
            pltpu.VMEM(wide, F32),
            pltpu.VMEM(wide, F32),
            pltpu.VMEM(wide, BF16),
            pltpu.VMEM(wide, BF16),
            pltpu.VMEM(wide, BF16),
            *states,
            *states,
            pltpu.VMEM((8, tokens), F32),
            pltpu.VMEM((head_n - 1, 8, tokens), F32),
            dma((6,)),
            dma((3 * heads,)),
            *state_sems,
            *state_sems,
            dma((head_n - 1,)),
            dma((head_n - 1,)),
        ],
        compiler_params=pltpu.CompilerParams(
            collective_id=0, has_side_effects=True, vmem_limit_bytes=48 * 2**20
        ),
        cost_estimate=pl.CostEstimate(
            flops=16 * heads * tokens * tokens * DIM,
            bytes_accessed=14 * tokens * local,
            transcendentals=heads * tokens * tokens,
        ),
    )(queries, keys, values, log_decay, gain.reshape(1, -1), upstream)


def solution(mesh):
    wide = P("ctx", "head")
    return jax.shard_map(
        on_device,
        mesh=mesh,
        in_specs=(wide, wide, wide, wide, P("head"), wide),
        out_specs=(wide, wide, wide),
        check_vma=False,
    )
```

time: 107 us -> 45 us (0.42)
  Pallas kernels: 0 us -> 36.6 us
  waiting for transfers between devices: 31.1 us -> 0 us
  matrix products: 24.4 us -> 0 us
  blocking collectives: 22.1 us -> 0 us
  between operations: 14.3 us -> 0.67 us
  other arithmetic: 4.23 us -> 0 us
  local copies, waits for them, and re-layouts: 9.88 us -> 7.39 us
    pallas_call x0 -> x1, Pallas kernels: none -> 36.6 us  [on_device(): pl.pallas_call(functools.partial(kernel, ctx_n, head_n, local * head_n),...]
    all_gather x2 -> x0, waiting for transfers between devices: 31 us -> none  [the longest x1 16.1 us: on_device(): lax.all_gather(slab_state[None], 'ctx', axis=0, tiled=True)]
    dot_general x16 -> x0, matrix products: 24.4 us -> none  [the longest x1 4.48 us: on_device(): jnp.einsum('nh,nhef->hef', back_weights, back_states, precision=HIGHEST)]
    psum x1 -> x0, blocking collectives: 11.9 us -> none  [on_device(): lax.psum((jnp.sum(attended * attended, axis=1), jnp.sum(scaled_grad * att...]
    all_gather x1 -> x0, blocking collectives: 10.2 us -> none  [on_device(): lax.all_gather(slab_level[None], 'ctx', axis=0, tiled=True)]
    reshape x3 -> x0, local copies, waits for them, and re-layouts: 2.44 us -> none  [the longest x1 1.32 us: on_device(): key_blocks = keys.reshape(block_shape)]
    another operation x2 -> x0, other arithmetic: 1.38 us -> none
    convert_element_type x1 -> x0, other arithmetic: 1.32 us -> none  [on_device(): grad_out = (inverse[:, None] * scaled_grad - attended * (inverse * invers...]
  transfers between devices with their start and end apart: 2 -> 0, of which waited for: 2 -> 0; matrix products, arithmetic and copies ran while one was open for 13% -> 0% of each run, Pallas kernels for 0% -> 0%
where the time goes in v1:
time: 45 us; the launch traced here: 44.7 us
  Pallas kernels  36.6 us (81%)
  local copies, waits for them, and re-layouts  7.39 us (16%)
  between operations  0.67 us (1%)
    pallas_call x1, Pallas kernels, on_device(): pl.pallas_call(functools.partial(kernel, ctx_n, head_n, local * head_n),...  36.6 us
    unnamed x14, local copies, waits for them, and re-layouts  7.39 us

profile of v1, /device:TPU:0, one launch (start us, length us, event | category | flops | bytes accessed | tf_op | source)
XLA Modules:
  0.0 44.7 jit_solution(11519480972083604238)
XLA Ops:
  0.6 0.0 copy-start.4
  0.6 0.8 %copy.9.ld_hbm = f32[512,4]{1,0:T(8,128)S(1)} copy(f32[512,4]{0,1:T(4,128)} %param.9) | data formatting | bytes 16384 | tf_op args[3]
  1.5 0.0 copy-done.4
  1.5 0.0 copy-start
  1.5 1.0 %copy-done = bf16[512,512]{1,0:T(8,128)(2,1)S(1)} copy-done((bf16[512,512]{1,0:T(8,128)(2,1)S(1)}, bf16[512,512]{1,0:T(8,128)(2,1)}, u32[]{:S(2)}) %copy-start) | copy-done | bytes 524312
  2.5 0.0 copy-start.1
  2.5 1.0 %copy-done.1 = bf16[512,512]{1,0:T(8,128)(2,1)S(1)} copy-done((bf16[512,512]{1,0:T(8,128)(2,1)S(1)}, bf16[512,512]{1,0:T(8,128)(2,1)}, u32[]{:S(2)}) %copy-start.1) | copy-done | bytes 524312
  3.6 0.0 copy-start.2
  3.6 1.0 %copy-done.2 = bf16[512,512]{1,0:T(8,128)(2,1)S(1)} copy-done((bf16[512,512]{1,0:T(8,128)(2,1)S(1)}, bf16[512,512]{1,0:T(8,128)(2,1)}, u32[]{:S(2)}) %copy-start.2) | copy-done | bytes 524312
  4.6 0.0 copy-start.3
  4.6 1.0 %copy-done.3 = bf16[512,512]{1,0:T(8,128)(2,1)S(1)} copy-done((bf16[512,512]{1,0:T(8,128)(2,1)S(1)}, bf16[512,512]{1,0:T(8,128)(2,1)}, u32[]{:S(2)}) %copy-start.3) | copy-done | bytes 524312
  5.7 36.6 %shard_map.85 = (bf16[512,512]{1,0:T(8,128)(2,1)S(1)}, bf16[512,512]{1,0:T(8,128)(2,1)S(1)}, bf16[512,512]{1,0:T(8,128)(2,1)S(1)}) custom-call(bf16[512,512]{1,0:T(8,128)(2,1)S(1)} %copy-done, bf16[512,512]{1,0:T(8,128)(2,1)S(1)} %copy-done.1, bf16[512,512]{1,0:T(8,128)(2,1)S(1)} %copy-done.2, f32[512,4]{1,0:T(8,128)S(1)} %copy.9.ld_hbm, ...), custom_call_target="tpu_custom_call" | custom-call | flops 2147483648 | bytes 3670016 | tf_op jit(solution)/shard_map/pallas_call | solution.py:361
  42.3 0.8 %copy.13 = bf16[512,512]{1,0:T(8,128)(2,1)} copy(bf16[512,512]{1,0:T(8,128)(2,1)S(1)} %get-tuple-element.6) | data formatting | bytes 1048576
  43.1 0.8 %copy.14 = bf16[512,512]{1,0:T(8,128)(2,1)} copy(bf16[512,512]{1,0:T(8,128)(2,1)S(1)} %get-tuple-element.7) | data formatting | bytes 1048576
  43.9 0.8 %copy.15 = bf16[512,512]{1,0:T(8,128)(2,1)} copy(bf16[512,512]{1,0:T(8,128)(2,1)S(1)} %get-tuple-element.8) | data formatting | bytes 1048576
Async XLA Ops:
  0.6 0.9 %copy-start.4 = (f32[512]{0:T(512)S(1)}, f32[512]{0:T(512)}, u32[]{:S(2)}) copy-start(f32[512]{0:T(512)} %param.10) | copy-start | bytes 6148
  1.5 1.0 %copy-start = (bf16[512,512]{1,0:T(8,128)(2,1)S(1)}, bf16[512,512]{1,0:T(8,128)(2,1)}, u32[]{:S(2)}) copy-start(bf16[512,512]{1,0:T(8,128)(2,1)} %q_hbm.1) | copy-start | bytes 1572868
  2.5 1.0 %copy-start.1 = (bf16[512,512]{1,0:T(8,128)(2,1)S(1)}, bf16[512,512]{1,0:T(8,128)(2,1)}, u32[]{:S(2)}) copy-start(bf16[512,512]{1,0:T(8,128)(2,1)} %k_hbm.1) | copy-start | bytes 1572868
  3.6 1.0 %copy-start.2 = (bf16[512,512]{1,0:T(8,128)(2,1)S(1)}, bf16[512,512]{1,0:T(8,128)(2,1)}, u32[]{:S(2)}) copy-start(bf16[512,512]{1,0:T(8,128)(2,1)} %v_hbm.1) | copy-start | bytes 1572868
  4.6 1.0 %copy-start.3 = (bf16[512,512]{1,0:T(8,128)(2,1)S(1)}, bf16[512,512]{1,0:T(8,128)(2,1)}, u32[]{:S(2)}) copy-start(bf16[512,512]{1,0:T(8,128)(2,1)} %up_hbm.1) | copy-start | bytes 1572868

commit v2 on v1

--- a/solution.py
+++ b/solution.py
@@ -32,16 +32,18 @@
     mix, dec, att, grad, wq, cum, cum_rows, dkp, dvp, dq, dk, dv,
     f_send, f_recv, f_tsend, f_trecv, f_pre,
     b_send, b_recv, b_tsend, b_trecv, b_pre,
-    z_send, z_recv,
+    z_send, z_recv, levels,
     in_sem, out_sem,
     fs_sem, fr_sem, fts_sem, ftr_sem, fps_sem, fpr_sem,
     bs_sem, br_sem, bts_sem, btr_sem, bps_sem, bpr_sem,
-    zs_sem, zr_sem,
+    zs_sem, zr_sem, ls_sem, lr_sem,
 ):
     tokens = q.shape[0]
     heads = q.shape[1] // DIM
     half = heads // 2
     bits = ctx_n.bit_length() - 1
+    bits_x = (bits - 1) // 2
+    chips_x = 2**bits_x
     tiles = tokens // TILE
     me = lax.axis_index("ctx")
     zed = lax.axis_index("head")
@@ -60,23 +62,39 @@
     load_ld, load_k, load_v, load_q, load_gain, load_up = loads
 
     barrier = pltpu.get_barrier_semaphore()
-    for b in range(bits):
-        pl.semaphore_signal(barrier, inc=1, device_id=(partners[b], zed), device_id_type=MESH)
+    for d in range(1, ctx_n):
+        pl.semaphore_signal(
+            barrier, inc=1, device_id=(lax.rem(me + d, ctx_n), zed), device_id_type=MESH
+        )
     for d in range(1, head_n):
         pl.semaphore_signal(
             barrier, inc=1, device_id=(me, lax.rem(zed + d, head_n)), device_id_type=MESH
         )
 
     load_ld.wait()
-    steps = jnp.pad(ld[...], ((0, 0), (0, DIM - heads)))
+    steps = jnp.pad(ld[...], ((0, 8 - heads), (0, 0)))
     row_id = lax.broadcasted_iota(jnp.int32, (tokens, tokens), 0)
     col_id = lax.broadcasted_iota(jnp.int32, (tokens, tokens), 1)
-    lower = jnp.where(row_id >= col_id, 1.0, 0.0).astype(BF16)
-    top, rest = split(steps)
-    low = (steps - top.astype(F32) - rest.astype(F32)).astype(BF16)
-    total_cum = dot(lower, top, (1, 0)) + (dot(lower, rest, (1, 0)) + dot(lower, low, (1, 0)))
-    cum[...] = total_cum
-    cum_rows[...] = total_cum.T[:8]
+    until = jnp.where(row_id <= col_id, 1.0, 0.0).astype(BF16)
+    top = steps.astype(BF16).astype(F32)
+    rest = (steps - top).astype(BF16).astype(F32)
+    parts = jnp.concatenate([top, rest, steps - top - rest, jnp.zeros_like(steps)], axis=0)
+    sums = dot(parts.astype(BF16), until, (1, 0))
+    rows_cum = sums[:8] + (sums[8:16] + sums[16:24])
+    cum_rows[...] = rows_cum
+    cum[...] = jnp.concatenate([rows_cum, jnp.zeros((DIM - 8, tokens), F32)], axis=0).T
+
+    levels[me] = jnp.broadcast_to(rows_cum[:, tokens - 1 :], (8, DIM))
+    pl.semaphore_wait(barrier, ctx_n + head_n - 2)
+    level_copies = []
+    for d in range(1, ctx_n):
+        copy = pltpu.make_async_remote_copy(
+            src_ref=levels.at[me], dst_ref=levels.at[me],
+            send_sem=ls_sem.at[d - 1], recv_sem=lr_sem.at[d - 1],
+            device_id=(lax.rem(me + d, ctx_n), zed), device_id_type=MESH,
+        )
+        copy.start()
+        level_copies.append(copy)
 
     def columns(h):
         return slice(h * DIM, (h + 1) * DIM)
@@ -86,9 +104,6 @@
 
     def total(h):
         return cum[tokens - 1 : tokens, h : h + 1]
-
-    def level_rows(h):
-        return jnp.broadcast_to(total(h), (8, DIM))
 
     diagonal = lax.broadcasted_iota(jnp.int32, (TILE, TILE), 0) >= lax.broadcasted_iota(
         jnp.int32, (TILE, TILE), 1
@@ -96,7 +111,9 @@
 
     def exchange(rev, send, recv, tsend, trecv, pre, ss, rs, tss, trs, pss, prs):
         pending = []
-        state = {}
+        spot = ctx_n - 1 - me if rev else me
+        chip = spot // 2
+        row_start = chip - lax.rem(chip, chips_x)
 
         def remote(src, dst, s_sem, r_sem, b):
             copy = pltpu.make_async_remote_copy(
@@ -107,64 +124,135 @@
             pending.append(copy)
             return copy
 
-        def upper(b):
-            return (1 - bit_values[b]) if rev else bit_values[b]
+        def span(first, last, o):
+            total_level = jnp.zeros((1, DIM), F32)
+            for j in range(ctx_n):
+                place = (ctx_n - 1 - j if rev else j) // 2
+                inside = jnp.logical_and(first <= place, place < last)
+                total_level = total_level + jnp.where(inside, levels[j, pl.ds(o, 1), :], 0.0)
+            return jnp.exp(total_level)
+
+        def is_upper(b):
+            return lax.rem(spot // (2**b), 2) == 1
 
         first = []
 
         def post(h, value):
-            send[h, :DIM] = value
-            send[h, DIM:] = level_rows(h)
+            send[h] = value
             first.append(remote(send.at[h], recv.at[h], ss.at[h], rs.at[h], 0))
 
-        def pair():
+        def slot_of(b, i, second):
+            return ((b - 1) * half + i) * 2 + second
+
+        copies = {}
+
+        def publish(b, i, value, second=0):
+            slot = slot_of(b, i, second)
+            tsend[slot] = value
+            copies[b, i, second] = remote(
+                tsend.at[slot], trecv.at[slot], tss.at[slot], trs.at[slot], b
+            )
+
+        def arrived(b, i, second=0):
+            copies[b, i, second].wait_recv()
+            return trecv[slot_of(b, i, second)]
+
+        def finish_head(i, value):
+            pre[own + i] = value
+            copies["pre", i] = remote(pre.at[own + i], pre.at[own + i], pss.at[i], prs.at[i], 0)
+
+        def pair(i):
+            o = own + i
+            first_level = jnp.exp(levels[me, pl.ds(o, 1), :])
+            other_level = jnp.exp(levels[partners[0], pl.ds(o, 1), :])
+            upper = is_upper(0)
+            return send[o] * jnp.where(upper, 1.0, other_level) + recv[o] * jnp.where(
+                upper, first_level, 1.0
+            )
+
+        def straight(i):
+            o = own + i
+            value = pair(i)
+            publish(1, i, value)
+            yield
+            before = jnp.zeros((DIM, DIM), F32)
+            for b in range(1, bits):
+                size = 2 ** (b - 1)
+                upper = is_upper(b)
+                other = arrived(b, i)
+                group = chip - lax.rem(chip, size)
+                before = before + jnp.where(upper, span(group, chip, o), 0.0) * other
+                if b + 1 < bits:
+                    upper_group = jnp.where(upper, group, group + size)
+                    faded = span(upper_group, upper_group + size, o)
+                    value = value * jnp.where(upper, 1.0, faded) + other * jnp.where(
+                        upper, faded, 1.0
+                    )
+                    publish(b + 1, i, value)
+                    yield
+            finish_head(i, before)
+            yield
+
+        def crossed(i):
+            o = own + i
+            value = pair(i)
+            column = value * span(chip + 1, row_start + chips_x, o)
+            publish(bits_x + 1, i, column)
+            yield
+            above = jnp.zeros((DIM, DIM), F32)
+            for b in range(bits_x + 1, bits):
+                size = 2 ** (b - 1)
+                upper = is_upper(b)
+                other = arrived(b, i)
+                group = chip - lax.rem(chip, size)
+                above = above + jnp.where(upper, span(group, row_start, o), 0.0) * other
+                if b + 1 < bits:
+                    upper_group = jnp.where(upper, group, group + size)
+                    faded = span(upper_group, upper_group + size, o)
+                    column = column * jnp.where(upper, 1.0, faded) + other * jnp.where(
+                        upper, faded, 1.0
+                    )
+                    publish(b + 1, i, column)
+                    yield
+            before = jnp.zeros((DIM, DIM), F32)
+            for b in range(1, bits_x + 1):
+                size = 2 ** (b - 1)
+                upper = is_upper(b)
+                group = chip - lax.rem(chip, size)
+                to_chip = jnp.where(upper, span(group, chip, o), 0.0)
+                if b < bits_x:
+                    publish(b, i, value)
+                    publish(b, i, above, 1)
+                    yield
+                    other = arrived(b, i)
+                    above = above + arrived(b, i, 1)
+                    before = before + to_chip * other
+                    upper_group = jnp.where(upper, group, group + size)
+                    faded = span(upper_group, upper_group + size, o)
+                    value = value * jnp.where(upper, 1.0, faded) + other * jnp.where(
+                        upper, faded, 1.0
+                    )
+                else:
+                    until_end = span(row_start, group + size, o)
+                    publish(b, i, jnp.where(upper, above, until_end * above + value))
+                    yield
+                    other = arrived(b, i)
+                    until_chip = span(row_start, chip, o)
+                    before = before + until_chip * above
+                    before = before + jnp.where(upper, to_chip, until_chip) * other
+            finish_head(i, before)
+            yield
+
+        routes = [straight(i) if i % 2 == 0 else crossed(i) for i in range(half)]
+
+        def advance():
+            for route in routes:
+                next(route)
+
+        def begin():
             for copy in first:
                 copy.wait_recv()
-            is_upper = upper(0) == 1
-            for i in range(half):
-                o = own + i
-                mine, other = send[o, :DIM], recv[o, :DIM]
-                my_level, other_level = send[o, DIM : DIM + 1], recv[o, DIM : DIM + 1]
-                value = mine * jnp.where(is_upper, 1.0, jnp.exp(other_level)) + other * jnp.where(
-                    is_upper, jnp.exp(my_level), 1.0
-                )
-                state[i] = (value, my_level + other_level, None, None)
-                publish(1, i)
-
-        copies = {}
-
-        def publish(b, i):
-            value, level, _, _ = state[i]
-            slot = (b - 1) * half + i
-            tsend[slot, :DIM] = value
-            tsend[slot, DIM:] = jnp.broadcast_to(level, (8, DIM))
-            copies[b, i] = remote(tsend.at[slot], trecv.at[slot], tss.at[slot], trs.at[slot], b)
-
-        def combine(b):
-            is_upper = upper(b) == 1
-            for i in range(half):
-                copies[b, i].wait_recv()
-                slot = (b - 1) * half + i
-                _, level, _, before_level = state[i]
-                value = tsend[slot, :DIM]
-                other, other_level = trecv[slot, :DIM], trecv[slot, DIM : DIM + 1]
-                if before_level is None:
-                    before = jnp.where(is_upper, other, 0.0)
-                    before_level = jnp.where(is_upper, other_level, 0.0)
-                else:
-                    before = pre[own + i] + jnp.where(is_upper, jnp.exp(before_level), 0.0) * other
-                    before_level = before_level + jnp.where(is_upper, other_level, 0.0)
-                pre[own + i] = before
-                if b + 1 < bits:
-                    value = value * jnp.where(is_upper, 1.0, jnp.exp(other_level)) + (
-                        other * jnp.where(is_upper, jnp.exp(level), 1.0)
-                    )
-                    state[i] = (value, level + other_level, None, before_level)
-                    publish(b + 1, i)
-                else:
-                    copies["pre", i] = remote(
-                        pre.at[own + i], pre.at[own + i], pss.at[i], prs.at[i], 0
-                    )
+            advance()
 
         def finish():
             for i in range(half):
@@ -174,11 +262,10 @@
 
         def result(h):
             outside = pre[h]
-            level = recv[h, DIM : DIM + 1]
-            return jnp.where(upper(0) == 1, outside * jnp.exp(level) + recv[h, :DIM], outside)
-
-        stages = [pair] + [functools.partial(combine, b) for b in range(1, bits)] + [finish]
-        return post, stages, result
+            level = jnp.exp(levels[partners[0], h : h + 1, :])
+            return jnp.where(is_upper(0), outside * level + recv[h], outside)
+
+        return post, [begin] + [advance] * (bits - 1) + [finish], result
 
     post, stages, start_state = exchange(
         False, f_send, f_recv, f_tsend, f_trecv, f_pre,
@@ -187,13 +274,10 @@
 
     load_k.wait()
     load_v.wait()
-    entered = bits + head_n - 1
     for h in range(heads):
         ending = jnp.exp(total(h) - cum_column(h))
         weighted_keys = (k[:, columns(h)].astype(F32) * ending).astype(BF16)
         value = dot(weighted_keys, v[:, columns(h)], (0, 0))
-        if h == 0:
-            pl.semaphore_wait(barrier, entered)
         post(h, value)
 
     load_q.wait()
@@ -226,7 +310,14 @@
             if place < len(stages):
                 stages[place]()
 
-    interleave([functools.partial(forward, h) for h in range(heads)], stages)
+    def forward_first():
+        forward(0)
+        for copy in level_copies:
+            copy.wait()
+
+    interleave(
+        [forward_first] + [functools.partial(forward, h) for h in range(1, heads)], stages
+    )
 
     load_gain.wait()
     load_up.wait()
@@ -339,11 +430,11 @@
     tokens, local = queries.shape
     heads = log_decay.shape[1]
     ctx_n, head_n = lax.axis_size("ctx"), lax.axis_size("head")
-    steps = ctx_n.bit_length() - 2
+    slots = (ctx_n.bit_length() - 2) * heads
     half = heads // 2
     wide = (tokens, local)
-    message = (heads, DIM + 8, DIM)
-    chip_message = (steps * half, DIM + 8, DIM)
+    message = (heads, DIM, DIM)
+    chip_message = (slots, DIM, DIM)
     states = [
         pltpu.VMEM(message, F32),
         pltpu.VMEM(message, F32),
@@ -353,21 +444,22 @@
     ]
     dma = pltpu.SemaphoreType.DMA
     state_sems = [
-        dma((heads,)), dma((heads,)), dma((steps * half,)), dma((steps * half,)),
+        dma((heads,)), dma((heads,)), dma((slots,)), dma((slots,)),
         dma((half,)), dma((half,)),
     ]
     anywhere = pl.BlockSpec(memory_space=pl.ANY)
+    in_hbm = pl.BlockSpec(memory_space=pltpu.HBM)
     out = jax.ShapeDtypeStruct(wide, BF16)
     return pl.pallas_call(
         functools.partial(kernel, ctx_n, head_n, local * head_n),
         out_shape=(out, out, out),
-        in_specs=[anywhere] * 6,
+        in_specs=[in_hbm] * 6,
         out_specs=(anywhere,) * 3,
         scratch_shapes=[
             pltpu.VMEM(wide, BF16),
             pltpu.VMEM(wide, BF16),
             pltpu.VMEM(wide, BF16),
-            pltpu.VMEM(log_decay.shape, F32),
+            pltpu.VMEM((heads, tokens), F32),
             pltpu.VMEM((1, local), F32),
             pltpu.VMEM(wide, BF16),
             pltpu.VMEM((heads, tokens, tokens), BF16),
@@ -386,22 +478,25 @@
             *states,
             pltpu.VMEM((8, tokens), F32),
             pltpu.VMEM((head_n - 1, 8, tokens), F32),
+            pltpu.VMEM((ctx_n, 8, DIM), F32),
             dma((6,)),
             dma((3 * heads,)),
             *state_sems,
             *state_sems,
             dma((head_n - 1,)),
             dma((head_n - 1,)),
+            dma((ctx_n - 1,)),
+            dma((ctx_n - 1,)),
         ],
         compiler_params=pltpu.CompilerParams(
-            collective_id=0, has_side_effects=True, vmem_limit_bytes=48 * 2**20
+            collective_id=0, has_side_effects=True, vmem_limit_bytes=60 * 2**20
         ),
         cost_estimate=pl.CostEstimate(
             flops=16 * heads * tokens * tokens * DIM,
             bytes_accessed=14 * tokens * local,
             transcendentals=heads * tokens * tokens,
         ),
-    )(queries, keys, values, log_decay, gain.reshape(1, -1), upstream)
+    )(queries, keys, values, log_decay.T, gain.reshape(1, -1), upstream)
 
 
 def solution(mesh):

time: 45 us -> 38.5 us (0.86)
  local copies, waits for them, and re-layouts: 7.39 us -> 3.95 us
  Pallas kernels: 36.6 us -> 33.7 us
    unnamed x14 -> x7, local copies, waits for them, and re-layouts: 7.39 us -> 3.95 us
    pallas_call x1, Pallas kernels: 36.6 us -> 33.7 us  [on_device(): pl.pallas_call(functools.partial(kernel, ctx_n, head_n, local * head_n),...]
where the time goes in v2:
time: 38.5 us; the launch traced here: 38.3 us
  Pallas kernels  33.7 us (88%)
  local copies, waits for them, and re-layouts  3.95 us (10%)
  between operations  0.65 us (2%)
    pallas_call x1, Pallas kernels, on_device(): pl.pallas_call(functools.partial(kernel, ctx_n, head_n, local * head_n),...  33.7 us
    unnamed x7, local copies, waits for them, and re-layouts  3.95 us

profile of v2, /device:TPU:0, one launch (start us, length us, event | category | flops | bytes accessed | tf_op | source)
XLA Modules:
  0.0 38.3 jit_solution(13406173292079071916)
XLA Ops:
  0.6 33.7 %shard_map.85 = (bf16[512,512]{1,0:T(8,128)(2,1)}, bf16[512,512]{1,0:T(8,128)(2,1)}, bf16[512,512]{1,0:T(8,128)(2,1)}) custom-call(bf16[512,512]{1,0:T(8,128)(2,1)} %q_hbm.1, bf16[512,512]{1,0:T(8,128)(2,1)} %k_hbm.1, bf16[512,512]{1,0:T(8,128)(2,1)} %v_hbm.1, f32[4,512]{1,0:T(4,128)} %bitcast.2, f32[1,512]{1,0:T(1,128)} %bitcast.3, bf16[512,512]{1,0:T(8,128)(2,1)} %up_hbm.1), custom_call_target="tpu_custom_call" | custom-call | flops 2147483648 | bytes 3670016 | tf_op jit(solution)/shard_map/pallas_call | solution.py:453
  34.3 0.0 copy-start.1
  34.3 1.9 %copy.12 = bf16[512,512]{1,0:T(8,128)(2,1)} copy(bf16[512,512]{1,0:T(8,128)(2,1)} %get-tuple-element.6) | data formatting | bytes 1048576
  36.3 0.0 copy-done.1
  36.3 0.0 copy-start
  36.3 0.8 %copy.13 = bf16[512,512]{1,0:T(8,128)(2,1)} copy(bf16[512,512]{1,0:T(8,128)(2,1)S(1)} %copy-done.1) | data formatting | bytes 1048576
  37.1 0.4 %copy-done = bf16[512,512]{1,0:T(8,128)(2,1)S(1)} copy-done((bf16[512,512]{1,0:T(8,128)(2,1)S(1)}, bf16[512,512]{1,0:T(8,128)(2,1)}, u32[]{:S(2)}) %copy-start) | copy-done | bytes 524312
  37.5 0.8 %copy.14 = bf16[512,512]{1,0:T(8,128)(2,1)} copy(bf16[512,512]{1,0:T(8,128)(2,1)S(1)} %copy-done) | data formatting | bytes 1048576
Async XLA Ops:
  34.3 1.9 %copy-start.1 = (bf16[512,512]{1,0:T(8,128)(2,1)S(1)}, bf16[512,512]{1,0:T(8,128)(2,1)}, u32[]{:S(2)}) copy-start(bf16[512,512]{1,0:T(8,128)(2,1)} %get-tuple-element.7) | copy-start | bytes 1572868
  36.3 1.2 %copy-start = (bf16[512,512]{1,0:T(8,128)(2,1)S(1)}, bf16[512,512]{1,0:T(8,128)(2,1)}, u32[]{:S(2)}) copy-start(bf16[512,512]{1,0:T(8,128)(2,1)} %get-tuple-element.8) | copy-start | bytes 1572868

commit v3 on v2

--- a/solution.py
+++ b/solution.py
@@ -9,6 +9,7 @@
 
 DIM = 128
 TILE = 256
+COPIES = 4
 EPSILON = 1e-06
 MESH = pl.DeviceIdType.MESH
 F32 = jnp.float32
@@ -71,11 +72,11 @@
             barrier, inc=1, device_id=(me, lax.rem(zed + d, head_n)), device_id_type=MESH
         )
 
-    load_ld.wait()
-    steps = jnp.pad(ld[...], ((0, 8 - heads), (0, 0)))
     row_id = lax.broadcasted_iota(jnp.int32, (tokens, tokens), 0)
     col_id = lax.broadcasted_iota(jnp.int32, (tokens, tokens), 1)
     until = jnp.where(row_id <= col_id, 1.0, 0.0).astype(BF16)
+    load_ld.wait()
+    steps = jnp.pad(ld[...], ((0, 8 - heads), (0, 0)))
     top = steps.astype(BF16).astype(F32)
     rest = (steps - top).astype(BF16).astype(F32)
     parts = jnp.concatenate([top, rest, steps - top - rest, jnp.zeros_like(steps)], axis=0)
@@ -275,49 +276,50 @@
     load_k.wait()
     load_v.wait()
     for h in range(heads):
-        ending = jnp.exp(total(h) - cum_column(h))
-        weighted_keys = (k[:, columns(h)].astype(F32) * ending).astype(BF16)
-        value = dot(weighted_keys, v[:, columns(h)], (0, 0))
-        post(h, value)
+        row = cum_rows[h : h + 1, :]
+        turned = k[:, columns(h)].T.astype(F32)
+        weighted_keys = (turned * jnp.exp(row[:, tokens - 1 :] - row)).astype(BF16)
+        post(h, dot(weighted_keys, v[:, columns(h)], (1, 0)))
 
     load_q.wait()
 
-    def forward(h):
-        for i in range(tiles):
-            rows = slice(i * TILE, (i + 1) * TILE)
-            total_rows = None
-            for j in range(i + 1):
-                sources = slice(j * TILE, (j + 1) * TILE)
-                scores = dot(q[rows, columns(h)], k[sources, columns(h)], (1, 1))
-                spread = cum[rows, h : h + 1] - cum_rows[h : h + 1, sources]
-                if i == j:
-                    spread = jnp.where(diagonal, spread, -1e30)
-                decays = jnp.exp(spread)
-                dec[h, rows, sources] = decays
-                mixing = (scores * decays).astype(BF16)
-                mix[h, rows, sources] = mixing
-                part = dot(mixing, v[sources, columns(h)], (1, 0))
-                total_rows = part if total_rows is None else total_rows + part
-            att[rows, columns(h)] = total_rows
-
-    def weigh_queries(h):
-        wq[:, columns(h)] = (q[:, columns(h)].astype(F32) * jnp.exp(cum_column(h))).astype(BF16)
+    def forward(h, i):
+        rows = slice(i * TILE, (i + 1) * TILE)
+        total_rows = None
+        for j in range(i + 1):
+            sources = slice(j * TILE, (j + 1) * TILE)
+            scores = dot(q[rows, columns(h)], k[sources, columns(h)], (1, 1))
+            spread = cum[rows, h : h + 1] - cum_rows[h : h + 1, sources]
+            if i == j:
+                spread = jnp.where(diagonal, spread, -1e30)
+            decays = jnp.exp(spread)
+            dec[h, rows, sources] = decays
+            mixing = (scores * decays).astype(BF16)
+            mix[h, sources, rows] = mixing.T
+            part = dot(mixing, v[sources, columns(h)], (1, 0))
+            total_rows = part if total_rows is None else total_rows + part
+        att[rows, columns(h)] = total_rows
+
+    def weigh_queries():
+        for h in range(heads):
+            turned = q[:, columns(h)].T.astype(F32)
+            wq[columns(h), :] = (turned * jnp.exp(cum_rows[h : h + 1, :])).astype(BF16)
+
+    def units(work):
+        return [functools.partial(work, h, i) for h in range(heads) for i in range(tiles)]
 
     def interleave(works, stages):
-        for place in range(max(len(works), len(stages))):
-            if place < len(works):
-                works[place]()
-            if place < len(stages):
-                stages[place]()
-
-    def forward_first():
-        forward(0)
+        for place, stage in enumerate(stages):
+            for work in works[place] if place < len(works) else ():
+                work()
+            stage()
+
+    def receive_levels():
         for copy in level_copies:
             copy.wait()
 
-    interleave(
-        [forward_first] + [functools.partial(forward, h) for h in range(1, heads)], stages
-    )
+    parts = units(forward)
+    interleave([parts[:2] + [receive_levels], parts[2:5], parts[5:], [weigh_queries]], stages)
 
     load_gain.wait()
     load_up.wait()
@@ -338,7 +340,7 @@
     cross_sum = jnp.sum(crosses, axis=1, keepdims=True)
     lane = lax.broadcasted_iota(jnp.int32, (tokens, DIM), 1)
     packed = jnp.where(lane == 0, square_sum, jnp.where(lane == 1, cross_sum, 0.0))
-    z_send[...] = packed.T[:8]
+    z_send[...] = packed.T[:2]
     z_copies = []
     for d in range(1, head_n):
         copy = pltpu.make_async_remote_copy(
@@ -348,13 +350,11 @@
         )
         copy.start()
         z_copies.append(copy)
-    for h in range(heads):
-        weigh_queries(h)
     sums = z_send[...]
     for d in range(1, head_n):
         z_copies[d - 1].wait_recv()
         sums = sums + z_recv[d - 1]
-    full = jnp.concatenate([sums, jnp.zeros((DIM - 8, tokens), F32)], axis=0).T
+    full = jnp.concatenate([sums, jnp.zeros((DIM - 2, tokens), F32)], axis=0).T
     square_sum, cross_sum = full[:, 0:1], full[:, 1:2]
     inverse = lax.rsqrt(square_sum / width + EPSILON)
     factor = inverse * inverse * inverse * cross_sum / width
@@ -367,7 +367,7 @@
         scaled = gain[:, columns(h)] * up[:, columns(h)].astype(F32)
         value = (inverse * scaled - att[:, columns(h)] * factor).astype(BF16)
         grad[:, columns(h)] = value
-        post(h, dot(wq[:, columns(h)], value, (0, 0)))
+        post(h, dot(wq[columns(h), :], value, (1, 0)))
     for copy in z_copies:
         copy.wait_send()
 
@@ -380,33 +380,33 @@
         copy.start()
         stores.append(copy)
 
-    def backward(h):
+    def backward(h, i):
         high, low = split(start_state(h))
         states = jnp.concatenate([high, low], axis=1)
-        key_sums, value_sums = [None] * tiles, [None] * tiles
-        for i in range(tiles):
-            rows = slice(i * TILE, (i + 1) * TILE)
-            grads = grad[rows, columns(h)]
-            query_sum = jnp.exp(cum[rows, h : h + 1]) * dot(
-                jnp.concatenate([grads, grads], axis=1), states, (1, 1)
-            )
-            for j in range(i + 1):
-                sources = slice(j * TILE, (j + 1) * TILE)
-                scores = dot(grads, v[sources, columns(h)], (1, 1))
-                mixing = (scores * dec[h, rows, sources]).astype(BF16)
-                query_sum = query_sum + dot(mixing, k[sources, columns(h)], (1, 0))
-                key_part = dot(mixing, q[rows, columns(h)], (0, 0))
-                value_part = dot(mix[h, rows, sources], grads, (0, 0))
-                key_sums[j] = key_part if i == j else key_sums[j] + key_part
-                value_sums[j] = value_part if i == j else value_sums[j] + value_part
-            dq[rows, columns(h)] = query_sum.astype(BF16)
-        store(0, h, dq, dq_out)
-        for j in range(tiles):
+        rows = slice(i * TILE, (i + 1) * TILE)
+        grads = grad[rows, columns(h)]
+        query_sum = jnp.exp(cum[rows, h : h + 1]) * dot(
+            jnp.concatenate([grads, grads], axis=1), states, (1, 1)
+        )
+        for j in range(i + 1):
             sources = slice(j * TILE, (j + 1) * TILE)
-            dkp[sources, columns(h)] = key_sums[j]
-            dvp[sources, columns(h)] = value_sums[j]
-
-    interleave([functools.partial(backward, h) for h in range(heads)], stages)
+            scores = dot(grads, v[sources, columns(h)], (1, 1))
+            mixing = (scores * dec[h, rows, sources]).astype(BF16)
+            query_sum = query_sum + dot(mixing, k[sources, columns(h)], (1, 0))
+            key_part = dot(mixing, q[rows, columns(h)], (0, 0))
+            value_part = dot(mix[h, sources, rows], grads, (1, 0))
+            if i == j:
+                dkp[sources, columns(h)] = key_part
+                dvp[sources, columns(h)] = value_part
+            else:
+                dkp[sources, columns(h)] += key_part
+                dvp[sources, columns(h)] += value_part
+        dq[rows, columns(h)] = query_sum.astype(BF16)
+        if i == tiles - 1:
+            store(0, h, dq, dq_out)
+
+    parts = units(backward)
+    interleave([parts[:2], parts[2:5], parts[5:7], parts[7:]], stages)
 
     for h in range(heads):
         high, low = split(end_state(h))
@@ -423,6 +423,23 @@
         dv[:, columns(h)] = (ending * value_carried + dvp[:, columns(h)]).astype(BF16)
         store(2, h, dv, dv_out)
     for copy in stores:
+        copy.wait()
+
+
+def hand_over(*refs):
+    count = (len(refs) - 1) // 2
+    sem = refs[-1]
+    copies = []
+    for i in range(count):
+        size = refs[i].shape[0] // COPIES
+        for part in range(COPIES):
+            rows = pl.ds(part * size, size)
+            copy = pltpu.make_async_copy(
+                refs[i].at[rows], refs[count + i].at[rows], sem.at[i * COPIES + part]
+            )
+            copy.start()
+            copies.append(copy)
+    for copy in copies:
         copy.wait()
 
 
@@ -450,7 +467,7 @@
     anywhere = pl.BlockSpec(memory_space=pl.ANY)
     in_hbm = pl.BlockSpec(memory_space=pltpu.HBM)
     out = jax.ShapeDtypeStruct(wide, BF16)
-    return pl.pallas_call(
+    results = pl.pallas_call(
         functools.partial(kernel, ctx_n, head_n, local * head_n),
         out_shape=(out, out, out),
         in_specs=[in_hbm] * 6,
@@ -466,7 +483,7 @@
             pltpu.VMEM((heads, tokens, tokens), F32),
             pltpu.VMEM(wide, F32),
             pltpu.VMEM(wide, BF16),
-            pltpu.VMEM(wide, BF16),
+            pltpu.VMEM((local, tokens), BF16),
             pltpu.VMEM((tokens, DIM), F32),
             pltpu.VMEM((8, tokens), F32),
             pltpu.VMEM(wide, F32),
@@ -476,8 +493,8 @@
             pltpu.VMEM(wide, BF16),
             *states,
             *states,
-            pltpu.VMEM((8, tokens), F32),
-            pltpu.VMEM((head_n - 1, 8, tokens), F32),
+            pltpu.VMEM((2, tokens), F32),
+            pltpu.VMEM((head_n - 1, 2, tokens), F32),
             pltpu.VMEM((ctx_n, 8, DIM), F32),
             dma((6,)),
             dma((3 * heads,)),
@@ -489,7 +506,7 @@
             dma((ctx_n - 1,)),
         ],
         compiler_params=pltpu.CompilerParams(
-            collective_id=0, has_side_effects=True, vmem_limit_bytes=60 * 2**20
+            collective_id=0, has_side_effects=True, vmem_limit_bytes=52 * 2**20
         ),
         cost_estimate=pl.CostEstimate(
             flops=16 * heads * tokens * tokens * DIM,
@@ -497,6 +514,13 @@
             transcendentals=heads * tokens * tokens,
         ),
     )(queries, keys, values, log_decay.T, gain.reshape(1, -1), upstream)
+    return pl.pallas_call(
+        hand_over,
+        out_shape=(out, out, out),
+        in_specs=[anywhere] * 3,
+        out_specs=(anywhere,) * 3,
+        scratch_shapes=[dma((3 * COPIES,))],
+    )(*results)
 
 
 def solution(mesh):

time: 38.5 us -> 87.8 us (2.28)
  Pallas kernels: 33.7 us -> 83.1 us
    pallas_call x0 -> x1, Pallas kernels: none -> 48.9 us  [on_device(): pl.pallas_call(hand_over, out_shape=(out, out, out), in_specs=[anywhere]...]
    unnamed x7 -> x10, local copies, waits for them, and re-layouts: 3.95 us -> 3.75 us
where the time goes in v3:
time: 87.8 us; the launch traced here: 87.5 us
  Pallas kernels  83.1 us (95%)
  local copies, waits for them, and re-layouts  3.75 us (4%)
    pallas_call x1, Pallas kernels, on_device(): pl.pallas_call(hand_over, out_shape=(out, out, out), in_specs=[anywhere]...  48.9 us
    pallas_call x1, Pallas kernels, on_device(): pl.pallas_call(functools.partial(kernel, ctx_n, head_n, local * head_n),...  34.3 us
    unnamed x10, local copies, waits for them, and re-layouts  3.75 us

profile of v3, /device:TPU:0, one launch (start us, length us, event | category | flops | bytes accessed | tf_op | source)
XLA Modules:
  0.0 87.5 jit_solution(6683877389651619536)
XLA Ops:
  0.6 0.0 copy-start.4
  0.6 0.7 copy-done.4
  1.3 0.0 copy-start.3
  1.3 0.7 copy-done.3
  2.0 34.3 %shard_map.85 = (bf16[512,512]{1,0:T(8,128)(2,1)S(1)}, bf16[512,512]{1,0:T(8,128)(2,1)S(1)}, bf16[512,512]{1,0:T(8,128)(2,1)S(1)}) custom-call(bf16[512,512]{1,0:T(8,128)(2,1)} %q_hbm.1, bf16[512,512]{1,0:T(8,128)(2,1)} %k_hbm.1, bf16[512,512]{1,0:T(8,128)(2,1)} %v_hbm.1, f32[4,512]{1,0:T(4,128)S(1)} %bitcast.2, f32[1,512]{1,0:T(1,128)S(1)} %bitcast.3, ...), custom_call_target="tpu_custom_call" | custom-call | flops 2147483648 | bytes 3670016 | tf_op jit(solution)/shard_map/pallas_call | solution.py:470
  36.3 0.0 copy-start
  36.3 0.8 copy-done
  37.1 0.0 copy-start.1
  37.1 0.8 copy-done.1
  37.9 0.0 copy-start.2
  37.9 0.8 copy-done.2
  38.7 48.9 %shard_map.86 = (bf16[512,512]{1,0:T(8,128)(2,1)}, bf16[512,512]{1,0:T(8,128)(2,1)}, bf16[512,512]{1,0:T(8,128)(2,1)}) custom-call(bf16[512,512]{1,0:T(8,128)(2,1)} %copy-done, bf16[512,512]{1,0:T(8,128)(2,1)} %copy-done.1, bf16[512,512]{1,0:T(8,128)(2,1)} %copy-done.2), custom_call_target="tpu_custom_call" | custom-call | tf_op jit(solution)/shard_map/pallas_call | solution.py:517
Async XLA Ops:
  0.6 0.7 copy-start.4
  1.3 0.7 copy-start.3
  36.3 0.8 copy-start
  37.1 0.8 copy-start.1
  37.9 0.8 copy-start.2

commit v4 on v3

--- a/solution.py
+++ b/solution.py
@@ -28,13 +28,13 @@
 def kernel(
     ctx_n, head_n, width,
     q_hbm, k_hbm, v_hbm, ld_hbm, gain_hbm, up_hbm,
-    dq_out, dk_out, dv_out,
+    dq, dk, dv,
     q, k, v, ld, gain, up,
-    mix, dec, att, grad, wq, cum, cum_rows, dkp, dvp, dq, dk, dv,
+    mix, dec, att, grad, wq, cum, cum_rows, dkp, dvp,
     f_send, f_recv, f_tsend, f_trecv, f_pre,
     b_send, b_recv, b_tsend, b_trecv, b_pre,
     z_send, z_recv, levels,
-    in_sem, out_sem,
+    in_sem,
     fs_sem, fr_sem, fts_sem, ftr_sem, fps_sem, fpr_sem,
     bs_sem, br_sem, bts_sem, btr_sem, bps_sem, bpr_sem,
     zs_sem, zr_sem, ls_sem, lr_sem,
@@ -371,15 +371,6 @@
     for copy in z_copies:
         copy.wait_send()
 
-    stores = []
-
-    def store(i, h, src, dst):
-        copy = pltpu.make_async_copy(
-            src.at[:, columns(h)], dst.at[:, columns(h)], out_sem.at[i * heads + h]
-        )
-        copy.start()
-        stores.append(copy)
-
     def backward(h, i):
         high, low = split(start_state(h))
         states = jnp.concatenate([high, low], axis=1)
@@ -402,8 +393,6 @@
                 dkp[sources, columns(h)] += key_part
                 dvp[sources, columns(h)] += value_part
         dq[rows, columns(h)] = query_sum.astype(BF16)
-        if i == tiles - 1:
-            store(0, h, dq, dq_out)
 
     parts = units(backward)
     interleave([parts[:2], parts[2:5], parts[5:7], parts[7:]], stages)
@@ -416,14 +405,10 @@
             jnp.concatenate([values, values], axis=1), jnp.concatenate([high, low], axis=1), (1, 1)
         )
         dk[:, columns(h)] = (ending * key_carried + dkp[:, columns(h)]).astype(BF16)
-        store(1, h, dk, dk_out)
         value_carried = dot(
             jnp.concatenate([keys, keys], axis=1), jnp.concatenate([high, low], axis=0), (1, 0)
         )
         dv[:, columns(h)] = (ending * value_carried + dvp[:, columns(h)]).astype(BF16)
-        store(2, h, dv, dv_out)
-    for copy in stores:
-        copy.wait()
 
 
 def hand_over(*refs):
@@ -464,14 +449,14 @@
         dma((heads,)), dma((heads,)), dma((slots,)), dma((slots,)),
         dma((half,)), dma((half,)),
     ]
-    anywhere = pl.BlockSpec(memory_space=pl.ANY)
+    in_vmem = pl.BlockSpec(memory_space=pltpu.VMEM)
     in_hbm = pl.BlockSpec(memory_space=pltpu.HBM)
     out = jax.ShapeDtypeStruct(wide, BF16)
     results = pl.pallas_call(
         functools.partial(kernel, ctx_n, head_n, local * head_n),
-        out_shape=(out, out, out),
+        out_shape=(pltpu.VMEM(wide, BF16),) * 3,
         in_specs=[in_hbm] * 6,
-        out_specs=(anywhere,) * 3,
+        out_specs=(in_vmem,) * 3,
         scratch_shapes=[
             pltpu.VMEM(wide, BF16),
             pltpu.VMEM(wide, BF16),
@@ -488,16 +473,12 @@
             pltpu.VMEM((8, tokens), F32),
             pltpu.VMEM(wide, F32),
             pltpu.VMEM(wide, F32),
-            pltpu.VMEM(wide, BF16),
-            pltpu.VMEM(wide, BF16),
-            pltpu.VMEM(wide, BF16),
             *states,
             *states,
             pltpu.VMEM((2, tokens), F32),
             pltpu.VMEM((head_n - 1, 2, tokens), F32),
             pltpu.VMEM((ctx_n, 8, DIM), F32),
             dma((6,)),
-            dma((3 * heads,)),
             *state_sems,
             *state_sems,
             dma((head_n - 1,)),
@@ -506,7 +487,7 @@
             dma((ctx_n - 1,)),
         ],
         compiler_params=pltpu.CompilerParams(
-            collective_id=0, has_side_effects=True, vmem_limit_bytes=52 * 2**20
+            collective_id=0, has_side_effects=True, vmem_limit_bytes=60 * 2**20
         ),
         cost_estimate=pl.CostEstimate(
             flops=16 * heads * tokens * tokens * DIM,
@@ -517,9 +498,10 @@
     return pl.pallas_call(
         hand_over,
         out_shape=(out, out, out),
-        in_specs=[anywhere] * 3,
-        out_specs=(anywhere,) * 3,
+        in_specs=[in_vmem] * 3,
+        out_specs=(in_hbm,) * 3,
         scratch_shapes=[dma((3 * COPIES,))],
+        compiler_params=pltpu.CompilerParams(vmem_limit_bytes=8 * 2**20),
     )(*results)
 
 

time: 87.8 us -> 34.3 us (0.39)
  Pallas kernels: 83.1 us -> 33.4 us
  local copies, waits for them, and re-layouts: 3.75 us -> 0 us
    pallas_call x1, Pallas kernels: 48.9 us -> 1.24 us  [on_device(): pl.pallas_call(hand_over, out_shape=(out, out, out), in_specs=[in_vmem] *...]
    unnamed x10 -> x0, local copies, waits for them, and re-layouts: 3.75 us -> none
    pallas_call x1, Pallas kernels: 34.3 us -> 32.2 us  [on_device(): pl.pallas_call(functools.partial(kernel, ctx_n, head_n, local * head_n),...]
where the time goes in v4:
time: 34.3 us; the launch traced here: 34 us
  Pallas kernels  33.4 us (97%)
  between operations  0.64 us (2%)
    pallas_call x1, Pallas kernels, on_device(): pl.pallas_call(functools.partial(kernel, ctx_n, head_n, local * head_n),...  32.2 us
    pallas_call x1, Pallas kernels, on_device(): pl.pallas_call(hand_over, out_shape=(out, out, out), in_specs=[in_vmem] *...  1.24 us

profile of v4, /device:TPU:0, one launch (start us, length us, event | category | flops | bytes accessed | tf_op | source)
XLA Modules:
  0.0 34.0 jit_solution(3504929660400600922)
XLA Ops:
  0.6 32.2 %shard_map.85 = (bf16[512,512]{1,0:T(8,128)(2,1)S(1)}, bf16[512,512]{1,0:T(8,128)(2,1)S(1)}, bf16[512,512]{1,0:T(8,128)(2,1)S(1)}) custom-call(bf16[512,512]{1,0:T(8,128)(2,1)} %q_hbm.1, bf16[512,512]{1,0:T(8,128)(2,1)} %k_hbm.1, bf16[512,512]{1,0:T(8,128)(2,1)} %v_hbm.1, f32[4,512]{1,0:T(4,128)} %bitcast.2, f32[1,512]{1,0:T(1,128)} %bitcast.3, ...), custom_call_target="tpu_custom_call" | custom-call | flops 2147483648 | bytes 3670016 | tf_op jit(solution)/shard_map/pallas_call | solution.py:455
  32.8 1.2 %shard_map.86 = (bf16[512,512]{1,0:T(8,128)(2,1)}, bf16[512,512]{1,0:T(8,128)(2,1)}, bf16[512,512]{1,0:T(8,128)(2,1)}) custom-call(bf16[512,512]{1,0:T(8,128)(2,1)S(1)} %get-tuple-element.6.refs_0_, bf16[512,512]{1,0:T(8,128)(2,1)S(1)} %get-tuple-element.7.refs_1_, bf16[512,512]{1,0:T(8,128)(2,1)S(1)} %get-tuple-element.8.refs_2_), custom_call_target="tpu_custom_call" | custom-call | tf_op jit(solution)/shard_map/pallas_call | solution.py:498

commit v5 on v4

--- a/solution.py
+++ b/solution.py
@@ -30,7 +30,7 @@
     q_hbm, k_hbm, v_hbm, ld_hbm, gain_hbm, up_hbm,
     dq, dk, dv,
     q, k, v, ld, gain, up,
-    mix, dec, att, grad, wq, cum, cum_rows, dkp, dvp,
+    mix, dec, att, grad, wq, cum, cum_rows, dkp, dvp, start_factor, end_factor, states,
     f_send, f_recv, f_tsend, f_trecv, f_pre,
     b_send, b_recv, b_tsend, b_trecv, b_pre,
     z_send, z_recv, levels,
@@ -100,12 +100,6 @@
     def columns(h):
         return slice(h * DIM, (h + 1) * DIM)
 
-    def cum_column(h):
-        return cum[:, h : h + 1]
-
-    def total(h):
-        return cum[tokens - 1 : tokens, h : h + 1]
-
     diagonal = lax.broadcasted_iota(jnp.int32, (TILE, TILE), 0) >= lax.broadcasted_iota(
         jnp.int32, (TILE, TILE), 1
     )
@@ -138,9 +132,9 @@
 
         first = []
 
-        def post(h, value):
+        def post(r, h, value):
             send[h] = value
-            first.append(remote(send.at[h], recv.at[h], ss.at[h], rs.at[h], 0))
+            first.append(remote(send.at[h], recv.at[h], ss.at[r], rs.at[r], 0))
 
         def slot_of(b, i, second):
             return ((b - 1) * half + i) * 2 + second
@@ -180,12 +174,13 @@
             for b in range(1, bits):
                 size = 2 ** (b - 1)
                 upper = is_upper(b)
+                group = chip - lax.rem(chip, size)
+                to_chip = jnp.where(upper, span(group, chip, o), 0.0)
+                upper_group = jnp.where(upper, group, group + size)
+                faded = span(upper_group, upper_group + size, o)
                 other = arrived(b, i)
-                group = chip - lax.rem(chip, size)
-                before = before + jnp.where(upper, span(group, chip, o), 0.0) * other
+                before = before + to_chip * other
                 if b + 1 < bits:
-                    upper_group = jnp.where(upper, group, group + size)
-                    faded = span(upper_group, upper_group + size, o)
                     value = value * jnp.where(upper, 1.0, faded) + other * jnp.where(
                         upper, faded, 1.0
                     )
@@ -204,12 +199,16 @@
             for b in range(bits_x + 1, bits):
                 size = 2 ** (b - 1)
                 upper = is_upper(b)
+                group = chip - lax.rem(chip, size)
+                to_row = jnp.where(upper, span(group, row_start, o), 0.0)
+                upper_group = jnp.where(upper, group, group + size)
+                faded = span(upper_group, upper_group + size, o)
+                if b + 1 == bits:
+                    last_group = chip - lax.rem(chip, chips_x // 2)
+                    until_end = span(row_start, last_group + chips_x // 2, o)
                 other = arrived(b, i)
-                group = chip - lax.rem(chip, size)
-                above = above + jnp.where(upper, span(group, row_start, o), 0.0) * other
+                above = above + to_row * other
                 if b + 1 < bits:
-                    upper_group = jnp.where(upper, group, group + size)
-                    faded = span(upper_group, upper_group + size, o)
                     column = column * jnp.where(upper, 1.0, faded) + other * jnp.where(
                         upper, faded, 1.0
                     )
@@ -234,12 +233,11 @@
                         upper, faded, 1.0
                     )
                 else:
-                    until_end = span(row_start, group + size, o)
                     publish(b, i, jnp.where(upper, above, until_end * above + value))
                     yield
-                    other = arrived(b, i)
                     until_chip = span(row_start, chip, o)
                     before = before + until_chip * above
+                    other = arrived(b, i)
                     before = before + jnp.where(upper, to_chip, until_chip) * other
             finish_head(i, before)
             yield
@@ -251,35 +249,45 @@
                 next(route)
 
         def begin():
-            for copy in first:
+            for copy in first[:half]:
                 copy.wait_recv()
             advance()
 
-        def finish():
+        def receive_rest():
+            for copy in first[half:]:
+                copy.wait_recv()
             for i in range(half):
                 copies["pre", i].wait_recv()
+
+        def finish():
             for copy in pending:
                 copy.wait_send()
 
         def result(h):
             outside = pre[h]
-            level = jnp.exp(levels[partners[0], h : h + 1, :])
+            level = jnp.exp(levels[partners[0], pl.ds(h, 1), :])
             return jnp.where(is_upper(0), outside * level + recv[h], outside)
 
-        return post, [begin] + [advance] * (bits - 1) + [finish], result
-
-    post, stages, start_state = exchange(
+        return post, [begin] + [advance] * (bits - 1), result, receive_rest, finish
+
+    other_first = [lax.rem(own + half + r, heads) for r in range(heads)]
+    own_first = [lax.rem(own + r, heads) for r in range(heads)]
+
+    def spot_columns(h):
+        return pl.ds(pl.multiple_of(h * DIM, DIM), DIM)
+
+    post, stages, start_state, receive_rest, finish_forward = exchange(
         False, f_send, f_recv, f_tsend, f_trecv, f_pre,
         fs_sem, fr_sem, fts_sem, ftr_sem, fps_sem, fpr_sem,
     )
 
     load_k.wait()
     load_v.wait()
-    for h in range(heads):
-        row = cum_rows[h : h + 1, :]
-        turned = k[:, columns(h)].T.astype(F32)
+    for r, h in enumerate(other_first):
+        row = cum_rows[pl.ds(h, 1), :]
+        turned = k[:, spot_columns(h)].T.astype(F32)
         weighted_keys = (turned * jnp.exp(row[:, tokens - 1 :] - row)).astype(BF16)
-        post(h, dot(weighted_keys, v[:, columns(h)], (1, 0)))
+        post(r, h, dot(weighted_keys, v[:, spot_columns(h)], (1, 0)))
 
     load_q.wait()
 
@@ -318,24 +326,35 @@
         for copy in level_copies:
             copy.wait()
 
+    def spread_factors():
+        starting = jnp.exp(cum[...])
+        ending = jnp.exp(cum[tokens - 1 : tokens, :] - cum[...])
+        for h in range(heads):
+            start_factor[h] = jnp.broadcast_to(starting[:, h : h + 1], (tokens, DIM))
+            end_factor[h] = jnp.broadcast_to(ending[:, h : h + 1], (tokens, DIM))
+
     parts = units(forward)
-    interleave([parts[:2] + [receive_levels], parts[2:5], parts[5:], [weigh_queries]], stages)
+    middle = len(parts) // 2
+    interleave([[receive_levels], parts[:middle], [spread_factors] + parts[middle:]], stages)
 
     load_gain.wait()
     load_up.wait()
-    squares = None
-    for h in range(heads):
+    for r, h in enumerate(own_first):
+        if r == half:
+            receive_rest()
+        at = spot_columns(h)
         high, low = split(start_state(h))
-        queries = q[:, columns(h)]
+        states[h] = jnp.concatenate([high, low], axis=1)
+        queries = q[:, at]
         carried = dot(
             jnp.concatenate([queries, queries], axis=1), jnp.concatenate([high, low], axis=0), (1, 0)
         )
-        value = att[:, columns(h)] + jnp.exp(cum_column(h)) * carried
-        att[:, columns(h)] = value
-        scaled = gain[:, columns(h)] * up[:, columns(h)].astype(F32)
+        value = att[:, at] + start_factor[h] * carried
+        att[:, at] = value
+        scaled = gain[:, at] * up[:, at].astype(F32)
         square, cross = value * value, scaled * value
-        squares = square if squares is None else squares + square
-        crosses = cross if h == 0 else crosses + cross
+        squares = square if r == 0 else squares + square
+        crosses = cross if r == 0 else crosses + cross
     square_sum = jnp.sum(squares, axis=1, keepdims=True)
     cross_sum = jnp.sum(crosses, axis=1, keepdims=True)
     lane = lax.broadcasted_iota(jnp.int32, (tokens, DIM), 1)
@@ -350,34 +369,36 @@
         )
         copy.start()
         z_copies.append(copy)
+    weigh_queries()
+    finish_forward()
     sums = z_send[...]
     for d in range(1, head_n):
         z_copies[d - 1].wait_recv()
         sums = sums + z_recv[d - 1]
-    full = jnp.concatenate([sums, jnp.zeros((DIM - 2, tokens), F32)], axis=0).T
-    square_sum, cross_sum = full[:, 0:1], full[:, 1:2]
-    inverse = lax.rsqrt(square_sum / width + EPSILON)
-    factor = inverse * inverse * inverse * cross_sum / width
-
-    post, stages, end_state = exchange(
+    inverse = lax.rsqrt(sums[0:1] / width + EPSILON)
+    factor = inverse * inverse * inverse * sums[1:2] / width
+    full = jnp.concatenate([inverse, factor, jnp.zeros((DIM - 2, tokens), F32)], axis=0).T
+    inverse = jnp.broadcast_to(full[:, 0:1], (tokens, DIM))
+    factor = jnp.broadcast_to(full[:, 1:2], (tokens, DIM))
+
+    post, stages, end_state, receive_rest, finish_backward = exchange(
         True, b_send, b_recv, b_tsend, b_trecv, b_pre,
         bs_sem, br_sem, bts_sem, btr_sem, bps_sem, bpr_sem,
     )
-    for h in range(heads):
-        scaled = gain[:, columns(h)] * up[:, columns(h)].astype(F32)
-        value = (inverse * scaled - att[:, columns(h)] * factor).astype(BF16)
-        grad[:, columns(h)] = value
-        post(h, dot(wq[columns(h), :], value, (1, 0)))
+    for r, h in enumerate(other_first):
+        at = spot_columns(h)
+        scaled = gain[:, at] * up[:, at].astype(F32)
+        value = (inverse * scaled - att[:, at] * factor).astype(BF16)
+        grad[:, at] = value
+        post(r, h, dot(wq[at, :], value, (1, 0)))
     for copy in z_copies:
         copy.wait_send()
 
     def backward(h, i):
-        high, low = split(start_state(h))
-        states = jnp.concatenate([high, low], axis=1)
         rows = slice(i * TILE, (i + 1) * TILE)
         grads = grad[rows, columns(h)]
-        query_sum = jnp.exp(cum[rows, h : h + 1]) * dot(
-            jnp.concatenate([grads, grads], axis=1), states, (1, 1)
+        query_sum = start_factor[h, rows] * dot(
+            jnp.concatenate([grads, grads], axis=1), states[h], (1, 1)
         )
         for j in range(i + 1):
             sources = slice(j * TILE, (j + 1) * TILE)
@@ -395,20 +416,24 @@
         dq[rows, columns(h)] = query_sum.astype(BF16)
 
     parts = units(backward)
-    interleave([parts[:2], parts[2:5], parts[5:7], parts[7:]], stages)
-
-    for h in range(heads):
+    interleave([[], parts[:middle], parts[middle:]], stages)
+
+    for r, h in enumerate(own_first):
+        if r == half:
+            receive_rest()
+        at = spot_columns(h)
         high, low = split(end_state(h))
-        ending = jnp.exp(total(h) - cum_column(h))
-        keys, values = k[:, columns(h)], v[:, columns(h)]
+        ending = end_factor[h]
+        keys, values = k[:, at], v[:, at]
         key_carried = dot(
             jnp.concatenate([values, values], axis=1), jnp.concatenate([high, low], axis=1), (1, 1)
         )
-        dk[:, columns(h)] = (ending * key_carried + dkp[:, columns(h)]).astype(BF16)
+        dk[:, at] = (ending * key_carried + dkp[:, at]).astype(BF16)
         value_carried = dot(
             jnp.concatenate([keys, keys], axis=1), jnp.concatenate([high, low], axis=0), (1, 0)
         )
-        dv[:, columns(h)] = (ending * value_carried + dvp[:, columns(h)]).astype(BF16)
+        dv[:, at] = (ending * value_carried + dvp[:, at]).astype(BF16)
+    finish_backward()
 
 
 def hand_over(*refs):
@@ -473,6 +498,9 @@
             pltpu.VMEM((8, tokens), F32),
             pltpu.VMEM(wide, F32),
             pltpu.VMEM(wide, F32),
+            pltpu.VMEM((heads, tokens, DIM), F32),
+            pltpu.VMEM((heads, tokens, DIM), F32),
+            pltpu.VMEM((heads, DIM, 2 * DIM), BF16),
             *states,
             *states,
             pltpu.VMEM((2, tokens), F32),

time: 34.3 us -> 32.9 us (0.959)
  Pallas kernels: 33.4 us -> 31.7 us
    pallas_call x1, Pallas kernels: 32.2 us -> 30.5 us  [on_device(): pl.pallas_call(functools.partial(kernel, ctx_n, head_n, local * head_n),...]
where the time goes in v5:
time: 32.9 us; the launch traced here: 32.3 us
  Pallas kernels  31.7 us (96%)
  between operations  0.64 us (2%)
    pallas_call x1, Pallas kernels, on_device(): pl.pallas_call(functools.partial(kernel, ctx_n, head_n, local * head_n),...  30.5 us
    pallas_call x1, Pallas kernels, on_device(): pl.pallas_call(hand_over, out_shape=(out, out, out), in_specs=[in_vmem] *...  1.24 us

profile of v5, /device:TPU:0, one launch (start us, length us, event | category | flops | bytes accessed | tf_op | source)
XLA Modules:
  0.0 32.3 jit_solution(5514258120096727256)
XLA Ops:
  0.6 30.5 %shard_map.85 = (bf16[512,512]{1,0:T(8,128)(2,1)S(1)}, bf16[512,512]{1,0:T(8,128)(2,1)S(1)}, bf16[512,512]{1,0:T(8,128)(2,1)S(1)}) custom-call(bf16[512,512]{1,0:T(8,128)(2,1)} %q_hbm.1, bf16[512,512]{1,0:T(8,128)(2,1)} %k_hbm.1, bf16[512,512]{1,0:T(8,128)(2,1)} %v_hbm.1, f32[4,512]{1,0:T(4,128)} %bitcast.2, f32[1,512]{1,0:T(1,128)} %bitcast.3, ...), custom_call_target="tpu_custom_call" | custom-call | flops 2147483648 | bytes 3670016 | tf_op jit(solution)/shard_map/pallas_call | solution.py:480
  31.1 1.2 %shard_map.86 = (bf16[512,512]{1,0:T(8,128)(2,1)}, bf16[512,512]{1,0:T(8,128)(2,1)}, bf16[512,512]{1,0:T(8,128)(2,1)}) custom-call(bf16[512,512]{1,0:T(8,128)(2,1)S(1)} %get-tuple-element.6.refs_0_, bf16[512,512]{1,0:T(8,128)(2,1)S(1)} %get-tuple-element.7.refs_1_, bf16[512,512]{1,0:T(8,128)(2,1)S(1)} %get-tuple-element.8.refs_2_), custom_call_target="tpu_custom_call" | custom-call | tf_op jit(solution)/shard_map/pallas_call | solution.py:526

commit v6 on v5

--- a/solution.py
+++ b/solution.py
@@ -10,6 +10,7 @@
 DIM = 128
 TILE = 256
 COPIES = 4
+PARTS = 2
 EPSILON = 1e-06
 MESH = pl.DeviceIdType.MESH
 F32 = jnp.float32
@@ -30,7 +31,7 @@
     q_hbm, k_hbm, v_hbm, ld_hbm, gain_hbm, up_hbm,
     dq, dk, dv,
     q, k, v, ld, gain, up,
-    mix, dec, att, grad, wq, cum, cum_rows, dkp, dvp, start_factor, end_factor, states,
+    mix, dec, att, grad, wq, cum, cum_rows, dkp, dvp, start_factor, end_factor, states, qt, dkt,
     f_send, f_recv, f_tsend, f_trecv, f_pre,
     b_send, b_recv, b_tsend, b_trecv, b_pre,
     z_send, z_recv, levels,
@@ -53,14 +54,28 @@
     bit_values = [lax.rem(me // (2**b), 2) for b in range(bits)]
     partners = [me + (2**b) * (1 - 2 * bit_values[b]) for b in range(bits)]
 
-    loads = []
-    for i, (src, dst) in enumerate(
-        ((ld_hbm, ld), (k_hbm, k), (v_hbm, v), (q_hbm, q), (gain_hbm, gain), (up_hbm, up))
-    ):
-        load = pltpu.make_async_copy(src, dst, in_sem.at[i])
-        load.start()
-        loads.append(load)
-    load_ld, load_k, load_v, load_q, load_gain, load_up = loads
+    def load(number, src, dst, parts):
+        size = src.shape[0] // parts
+        copies = []
+        for part in range(parts):
+            rows = pl.ds(part * size, size)
+            copy = pltpu.make_async_copy(
+                src.at[rows], dst.at[rows], in_sem.at[number * COPIES + part]
+            )
+            copy.start()
+            copies.append(copy)
+        return copies
+
+    def wait(copies):
+        for copy in copies:
+            copy.wait()
+
+    load_ld = load(0, ld_hbm, ld, 1)
+    load_k = load(1, k_hbm, k, COPIES)
+    load_v = load(2, v_hbm, v, COPIES)
+    load_q = load(3, q_hbm, q, COPIES)
+    load_gain = load(4, gain_hbm, gain, 1)
+    load_up = load(5, up_hbm, up, COPIES)
 
     barrier = pltpu.get_barrier_semaphore()
     for d in range(1, ctx_n):
@@ -75,7 +90,7 @@
     row_id = lax.broadcasted_iota(jnp.int32, (tokens, tokens), 0)
     col_id = lax.broadcasted_iota(jnp.int32, (tokens, tokens), 1)
     until = jnp.where(row_id <= col_id, 1.0, 0.0).astype(BF16)
-    load_ld.wait()
+    wait(load_ld)
     steps = jnp.pad(ld[...], ((0, 8 - heads), (0, 0)))
     top = steps.astype(BF16).astype(F32)
     rest = (steps - top).astype(BF16).astype(F32)
@@ -137,7 +152,8 @@
             first.append(remote(send.at[h], recv.at[h], ss.at[r], rs.at[r], 0))
 
         def slot_of(b, i, second):
-            return ((b - 1) * half + i) * 2 + second
+            head, part = i
+            return (((b - 1) * half + head) * PARTS + part) * 2 + second
 
         copies = {}
 
@@ -152,25 +168,30 @@
             copies[b, i, second].wait_recv()
             return trecv[slot_of(b, i, second)]
 
+        def rows_of(i):
+            return pl.ds(i[1] * (DIM // PARTS), DIM // PARTS)
+
         def finish_head(i, value):
-            pre[own + i] = value
-            copies["pre", i] = remote(pre.at[own + i], pre.at[own + i], pss.at[i], prs.at[i], 0)
+            at = (own + i[0], rows_of(i))
+            number = i[0] * PARTS + i[1]
+            pre[at] = value
+            copies["pre", i] = remote(pre.at[at], pre.at[at], pss.at[number], prs.at[number], 0)
 
         def pair(i):
-            o = own + i
+            o, rows = own + i[0], rows_of(i)
             first_level = jnp.exp(levels[me, pl.ds(o, 1), :])
             other_level = jnp.exp(levels[partners[0], pl.ds(o, 1), :])
             upper = is_upper(0)
-            return send[o] * jnp.where(upper, 1.0, other_level) + recv[o] * jnp.where(
+            return send[o, rows] * jnp.where(upper, 1.0, other_level) + recv[o, rows] * jnp.where(
                 upper, first_level, 1.0
             )
 
         def straight(i):
-            o = own + i
+            o = own + i[0]
             value = pair(i)
             publish(1, i, value)
             yield
-            before = jnp.zeros((DIM, DIM), F32)
+            before = jnp.zeros((DIM // PARTS, DIM), F32)
             for b in range(1, bits):
                 size = 2 ** (b - 1)
                 upper = is_upper(b)
@@ -190,12 +211,12 @@
             yield
 
         def crossed(i):
-            o = own + i
+            o = own + i[0]
             value = pair(i)
             column = value * span(chip + 1, row_start + chips_x, o)
             publish(bits_x + 1, i, column)
             yield
-            above = jnp.zeros((DIM, DIM), F32)
+            above = jnp.zeros((DIM // PARTS, DIM), F32)
             for b in range(bits_x + 1, bits):
                 size = 2 ** (b - 1)
                 upper = is_upper(b)
@@ -214,7 +235,7 @@
                     )
                     publish(b + 1, i, column)
                     yield
-            before = jnp.zeros((DIM, DIM), F32)
+            before = jnp.zeros((DIM // PARTS, DIM), F32)
             for b in range(1, bits_x + 1):
                 size = 2 ** (b - 1)
                 upper = is_upper(b)
@@ -242,22 +263,27 @@
             finish_head(i, before)
             yield
 
-        routes = [straight(i) if i % 2 == 0 else crossed(i) for i in range(half)]
-
-        def advance():
-            for route in routes:
+        routes = [
+            [(crossed if i % 2 else straight)((i, part)) for i in range(half)]
+            for part in range(PARTS)
+        ]
+
+        def advance(part):
+            for route in routes[part]:
                 next(route)
 
         def begin():
             for copy in first[:half]:
                 copy.wait_recv()
-            advance()
+            for part in range(PARTS):
+                advance(part)
 
         def receive_rest():
             for copy in first[half:]:
                 copy.wait_recv()
             for i in range(half):
-                copies["pre", i].wait_recv()
+                for part in range(PARTS):
+                    copies["pre", (i, part)].wait_recv()
 
         def finish():
             for copy in pending:
@@ -268,7 +294,8 @@
             level = jnp.exp(levels[partners[0], pl.ds(h, 1), :])
             return jnp.where(is_upper(0), outside * level + recv[h], outside)
 
-        return post, [begin] + [advance] * (bits - 1), result, receive_rest, finish
+        steps = [functools.partial(advance, part) for part in range(PARTS)] * (bits - 1)
+        return post, [begin] + steps, result, receive_rest, finish
 
     other_first = [lax.rem(own + half + r, heads) for r in range(heads)]
     own_first = [lax.rem(own + r, heads) for r in range(heads)]
@@ -281,15 +308,15 @@
         fs_sem, fr_sem, fts_sem, ftr_sem, fps_sem, fpr_sem,
     )
 
-    load_k.wait()
-    load_v.wait()
+    wait(load_k)
+    wait(load_v)
     for r, h in enumerate(other_first):
         row = cum_rows[pl.ds(h, 1), :]
         turned = k[:, spot_columns(h)].T.astype(F32)
         weighted_keys = (turned * jnp.exp(row[:, tokens - 1 :] - row)).astype(BF16)
         post(r, h, dot(weighted_keys, v[:, spot_columns(h)], (1, 0)))
 
-    load_q.wait()
+    wait(load_q)
 
     def forward(h, i):
         rows = slice(i * TILE, (i + 1) * TILE)
@@ -311,6 +338,7 @@
     def weigh_queries():
         for h in range(heads):
             turned = q[:, columns(h)].T.astype(F32)
+            qt[columns(h), :] = turned.astype(BF16)
             wq[columns(h), :] = (turned * jnp.exp(cum_rows[h : h + 1, :])).astype(BF16)
 
     def units(work):
@@ -334,11 +362,11 @@
             end_factor[h] = jnp.broadcast_to(ending[:, h : h + 1], (tokens, DIM))
 
     parts = units(forward)
-    middle = len(parts) // 2
-    interleave([[receive_levels], parts[:middle], [spread_factors] + parts[middle:]], stages)
-
-    load_gain.wait()
-    load_up.wait()
+    shares = [parts[tiles * h : tiles * (h + 1)] for h in range(heads)]
+    interleave([[receive_levels]] + shares[:-1] + [[spread_factors] + shares[-1]], stages)
+
+    wait(load_gain)
+    wait(load_up)
     for r, h in enumerate(own_first):
         if r == half:
             receive_rest()
@@ -355,11 +383,11 @@
         square, cross = value * value, scaled * value
         squares = square if r == 0 else squares + square
         crosses = cross if r == 0 else crosses + cross
-    square_sum = jnp.sum(squares, axis=1, keepdims=True)
-    cross_sum = jnp.sum(crosses, axis=1, keepdims=True)
-    lane = lax.broadcasted_iota(jnp.int32, (tokens, DIM), 1)
-    packed = jnp.where(lane == 0, square_sum, jnp.where(lane == 1, cross_sum, 0.0))
-    z_send[...] = packed.T[:2]
+    ones = jnp.ones((16, 2 * DIM), BF16)
+    for place, addends in enumerate((squares, crosses)):
+        high, low = split(addends)
+        added = dot(ones, jnp.concatenate([high, low], axis=1), (1, 1))
+        z_send[place : place + 1] = added[:1]
     z_copies = []
     for d in range(1, head_n):
         copy = pltpu.make_async_remote_copy(
@@ -405,18 +433,21 @@
             scores = dot(grads, v[sources, columns(h)], (1, 1))
             mixing = (scores * dec[h, rows, sources]).astype(BF16)
             query_sum = query_sum + dot(mixing, k[sources, columns(h)], (1, 0))
-            key_part = dot(mixing, q[rows, columns(h)], (0, 0))
+            key_part = dot(qt[columns(h), rows], mixing, (1, 0))
             value_part = dot(mix[h, sources, rows], grads, (1, 0))
             if i == j:
-                dkp[sources, columns(h)] = key_part
+                dkt[columns(h), sources] = key_part
                 dvp[sources, columns(h)] = value_part
             else:
-                dkp[sources, columns(h)] += key_part
+                dkt[columns(h), sources] += key_part
                 dvp[sources, columns(h)] += value_part
         dq[rows, columns(h)] = query_sum.astype(BF16)
+        if i == tiles - 1:
+            dkp[:, columns(h)] = dkt[columns(h), :].T
 
     parts = units(backward)
-    interleave([[], parts[:middle], parts[middle:]], stages)
+    shares = [parts[tiles * h : tiles * (h + 1)] for h in range(heads)]
+    interleave([[]] + shares, stages)
 
     for r, h in enumerate(own_first):
         if r == half:
@@ -457,11 +488,11 @@
     tokens, local = queries.shape
     heads = log_decay.shape[1]
     ctx_n, head_n = lax.axis_size("ctx"), lax.axis_size("head")
-    slots = (ctx_n.bit_length() - 2) * heads
+    slots = (ctx_n.bit_length() - 2) * heads * PARTS
     half = heads // 2
     wide = (tokens, local)
     message = (heads, DIM, DIM)
-    chip_message = (slots, DIM, DIM)
+    chip_message = (slots, DIM // PARTS, DIM)
     states = [
         pltpu.VMEM(message, F32),
         pltpu.VMEM(message, F32),
@@ -472,7 +503,7 @@
     dma = pltpu.SemaphoreType.DMA
     state_sems = [
         dma((heads,)), dma((heads,)), dma((slots,)), dma((slots,)),
-        dma((half,)), dma((half,)),
+        dma((half * PARTS,)), dma((half * PARTS,)),
     ]
     in_vmem = pl.BlockSpec(memory_space=pltpu.VMEM)
     in_hbm = pl.BlockSpec(memory_space=pltpu.HBM)
@@ -501,12 +532,14 @@
             pltpu.VMEM((heads, tokens, DIM), F32),
             pltpu.VMEM((heads, tokens, DIM), F32),
             pltpu.VMEM((heads, DIM, 2 * DIM), BF16),
+            pltpu.VMEM((local, tokens), BF16),
+            pltpu.VMEM((local, tokens), F32),
             *states,
             *states,
             pltpu.VMEM((2, tokens), F32),
             pltpu.VMEM((head_n - 1, 2, tokens), F32),
             pltpu.VMEM((ctx_n, 8, DIM), F32),
-            dma((6,)),
+            dma((6 * COPIES,)),
             *state_sems,
             *state_sems,
             dma((head_n - 1,)),

time: 32.9 us -> 34 us (1.033)
  Pallas kernels: 31.7 us -> 32.9 us
    pallas_call x1, Pallas kernels: 30.5 us -> 31.6 us  [on_device(): pl.pallas_call(functools.partial(kernel, ctx_n, head_n, local * head_n),...]
where the time goes in v6:
time: 34 us; the launch traced here: 33.5 us
  Pallas kernels  32.9 us (97%)
  between operations  0.64 us (2%)
    pallas_call x1, Pallas kernels, on_device(): pl.pallas_call(functools.partial(kernel, ctx_n, head_n, local * head_n),...  31.6 us
    pallas_call x1, Pallas kernels, on_device(): pl.pallas_call(hand_over, out_shape=(out, out, out), in_specs=[in_vmem] *...  1.24 us

profile of v6, /device:TPU:0, one launch (start us, length us, event | category | flops | bytes accessed | tf_op | source)
XLA Modules:
  0.0 33.5 jit_solution(502617897548750108)
XLA Ops:
  0.6 31.6 %shard_map.85 = (bf16[512,512]{1,0:T(8,128)(2,1)S(1)}, bf16[512,512]{1,0:T(8,128)(2,1)S(1)}, bf16[512,512]{1,0:T(8,128)(2,1)S(1)}) custom-call(bf16[512,512]{1,0:T(8,128)(2,1)} %q_hbm.1, bf16[512,512]{1,0:T(8,128)(2,1)} %k_hbm.1, bf16[512,512]{1,0:T(8,128)(2,1)} %v_hbm.1, f32[4,512]{1,0:T(4,128)} %bitcast.2, f32[1,512]{1,0:T(1,128)} %bitcast.3, ...), custom_call_target="tpu_custom_call" | custom-call | flops 2147483648 | bytes 3670016 | tf_op jit(solution)/shard_map/pallas_call | solution.py:511
  32.3 1.2 %shard_map.86 = (bf16[512,512]{1,0:T(8,128)(2,1)}, bf16[512,512]{1,0:T(8,128)(2,1)}, bf16[512,512]{1,0:T(8,128)(2,1)}) custom-call(bf16[512,512]{1,0:T(8,128)(2,1)S(1)} %get-tuple-element.6.refs_0_, bf16[512,512]{1,0:T(8,128)(2,1)S(1)} %get-tuple-element.7.refs_1_, bf16[512,512]{1,0:T(8,128)(2,1)S(1)} %get-tuple-element.8.refs_2_), custom_call_target="tpu_custom_call" | custom-call | tf_op jit(solution)/shard_map/pallas_call | solution.py:559

commit v7 on v6

--- a/solution.py
+++ b/solution.py
@@ -10,7 +10,7 @@
 DIM = 128
 TILE = 256
 COPIES = 4
-PARTS = 2
+PARTS = 1
 EPSILON = 1e-06
 MESH = pl.DeviceIdType.MESH
 F32 = jnp.float32
@@ -71,11 +71,8 @@
             copy.wait()
 
     load_ld = load(0, ld_hbm, ld, 1)
-    load_k = load(1, k_hbm, k, COPIES)
-    load_v = load(2, v_hbm, v, COPIES)
-    load_q = load(3, q_hbm, q, COPIES)
-    load_gain = load(4, gain_hbm, gain, 1)
-    load_up = load(5, up_hbm, up, COPIES)
+    load_k = load(1, k_hbm, k, 2)
+    load_v = load(2, v_hbm, v, 2)
 
     barrier = pltpu.get_barrier_semaphore()
     for d in range(1, ctx_n):
@@ -86,6 +83,10 @@
         pl.semaphore_signal(
             barrier, inc=1, device_id=(me, lax.rem(zed + d, head_n)), device_id_type=MESH
         )
+
+    load_q = load(3, q_hbm, q, 1)
+    load_gain = load(4, gain_hbm, gain, 1)
+    load_up = load(5, up_hbm, up, 1)
 
     row_id = lax.broadcasted_iota(jnp.int32, (tokens, tokens), 0)
     col_id = lax.broadcasted_iota(jnp.int32, (tokens, tokens), 1)
@@ -362,8 +363,8 @@
             end_factor[h] = jnp.broadcast_to(ending[:, h : h + 1], (tokens, DIM))
 
     parts = units(forward)
-    shares = [parts[tiles * h : tiles * (h + 1)] for h in range(heads)]
-    interleave([[receive_levels]] + shares[:-1] + [[spread_factors] + shares[-1]], stages)
+    middle = len(parts) // 2
+    interleave([[receive_levels], parts[:middle], [spread_factors] + parts[middle:]], stages)
 
     wait(load_gain)
     wait(load_up)
@@ -446,8 +447,7 @@
             dkp[:, columns(h)] = dkt[columns(h), :].T
 
     parts = units(backward)
-    shares = [parts[tiles * h : tiles * (h + 1)] for h in range(heads)]
-    interleave([[]] + shares, stages)
+    interleave([[], parts[:middle], parts[middle:]], stages)
 
     for r, h in enumerate(own_first):
         if r == half:

time: 34 us -> 33.1 us (0.974)
  Pallas kernels: 32.9 us -> 31.8 us
    pallas_call x1, Pallas kernels: 31.6 us -> 30.6 us  [on_device(): pl.pallas_call(functools.partial(kernel, ctx_n, head_n, local * head_n),...]
where the time goes in v7:
time: 33.1 us; the launch traced here: 32.5 us
  Pallas kernels  31.8 us (96%)
  between operations  0.64 us (2%)
    pallas_call x1, Pallas kernels, on_device(): pl.pallas_call(functools.partial(kernel, ctx_n, head_n, local * head_n),...  30.6 us
    pallas_call x1, Pallas kernels, on_device(): pl.pallas_call(hand_over, out_shape=(out, out, out), in_specs=[in_vmem] *...  1.24 us

profile of v7, /device:TPU:0, one launch (start us, length us, event | category | flops | bytes accessed | tf_op | source)
XLA Modules:
  0.0 32.5 jit_solution(14026022104242954919)
XLA Ops:
  0.6 30.6 %shard_map.85 = (bf16[512,512]{1,0:T(8,128)(2,1)S(1)}, bf16[512,512]{1,0:T(8,128)(2,1)S(1)}, bf16[512,512]{1,0:T(8,128)(2,1)S(1)}) custom-call(bf16[512,512]{1,0:T(8,128)(2,1)} %q_hbm.1, bf16[512,512]{1,0:T(8,128)(2,1)} %k_hbm.1, bf16[512,512]{1,0:T(8,128)(2,1)} %v_hbm.1, f32[4,512]{1,0:T(4,128)} %bitcast.2, f32[1,512]{1,0:T(1,128)} %bitcast.3, ...), custom_call_target="tpu_custom_call" | custom-call | flops 2147483648 | bytes 3670016 | tf_op jit(solution)/shard_map/pallas_call | solution.py:511
  31.2 1.2 %shard_map.86 = (bf16[512,512]{1,0:T(8,128)(2,1)}, bf16[512,512]{1,0:T(8,128)(2,1)}, bf16[512,512]{1,0:T(8,128)(2,1)}) custom-call(bf16[512,512]{1,0:T(8,128)(2,1)S(1)} %get-tuple-element.6.refs_0_, bf16[512,512]{1,0:T(8,128)(2,1)S(1)} %get-tuple-element.7.refs_1_, bf16[512,512]{1,0:T(8,128)(2,1)S(1)} %get-tuple-element.8.refs_2_), custom_call_target="tpu_custom_call" | custom-call | tf_op jit(solution)/shard_map/pallas_call | solution.py:559

commit v8 on v7

--- a/solution.py
+++ b/solution.py
@@ -368,58 +368,84 @@
 
     wait(load_gain)
     wait(load_up)
-    for r, h in enumerate(own_first):
-        if r == half:
-            receive_rest()
-        at = spot_columns(h)
+    squares, crosses = [None] * tiles, [None] * tiles
+
+    def hold_state(h):
         high, low = split(start_state(h))
         states[h] = jnp.concatenate([high, low], axis=1)
-        queries = q[:, at]
+
+    def carry(h, i):
+        at, rows = spot_columns(h), slice(i * TILE, (i + 1) * TILE)
+        queries = q[rows, at]
+        halves = states[h]
         carried = dot(
-            jnp.concatenate([queries, queries], axis=1), jnp.concatenate([high, low], axis=0), (1, 0)
+            jnp.concatenate([queries, queries], axis=1),
+            jnp.concatenate([halves[:, :DIM], halves[:, DIM:]], axis=0),
+            (1, 0),
         )
-        value = att[:, at] + start_factor[h] * carried
-        att[:, at] = value
-        scaled = gain[:, at] * up[:, at].astype(F32)
+        value = att[rows, at] + start_factor[h, rows] * carried
+        att[rows, at] = value
+        scaled = gain[:, at] * up[rows, at].astype(F32)
         square, cross = value * value, scaled * value
-        squares = square if r == 0 else squares + square
-        crosses = cross if r == 0 else crosses + cross
-    ones = jnp.ones((16, 2 * DIM), BF16)
-    for place, addends in enumerate((squares, crosses)):
-        high, low = split(addends)
-        added = dot(ones, jnp.concatenate([high, low], axis=1), (1, 1))
-        z_send[place : place + 1] = added[:1]
+        squares[i] = square if squares[i] is None else squares[i] + square
+        crosses[i] = cross if crosses[i] is None else crosses[i] + cross
+
     z_copies = []
-    for d in range(1, head_n):
-        copy = pltpu.make_async_remote_copy(
-            src_ref=z_send, dst_ref=z_recv.at[d - 1],
-            send_sem=zs_sem.at[d - 1], recv_sem=zr_sem.at[d - 1],
-            device_id=(me, lax.rem(zed + d, head_n)), device_id_type=MESH,
-        )
-        copy.start()
-        z_copies.append(copy)
+
+    def send_sums(i):
+        ones = jnp.ones((16, 2 * DIM), BF16)
+        for place, addends in enumerate((squares[i], crosses[i])):
+            high, low = split(addends)
+            added = dot(ones, jnp.concatenate([high, low], axis=1), (1, 1))
+            z_send[i, place : place + 1] = added[:1]
+        for d in range(1, head_n):
+            number = i * (head_n - 1) + d - 1
+            copy = pltpu.make_async_remote_copy(
+                src_ref=z_send.at[i], dst_ref=z_recv.at[number],
+                send_sem=zs_sem.at[number], recv_sem=zr_sem.at[number],
+                device_id=(me, lax.rem(zed + d, head_n)), device_id_type=MESH,
+            )
+            copy.start()
+            z_copies.append(copy)
+
+    for h in own_first[:half]:
+        hold_state(h)
+        for i in range(tiles):
+            carry(h, i)
+    receive_rest()
+    for h in own_first[half:]:
+        hold_state(h)
+    for i in range(tiles):
+        for h in own_first[half:]:
+            carry(h, i)
+        send_sums(i)
     weigh_queries()
     finish_forward()
-    sums = z_send[...]
-    for d in range(1, head_n):
-        z_copies[d - 1].wait_recv()
-        sums = sums + z_recv[d - 1]
-    inverse = lax.rsqrt(sums[0:1] / width + EPSILON)
-    factor = inverse * inverse * inverse * sums[1:2] / width
-    full = jnp.concatenate([inverse, factor, jnp.zeros((DIM - 2, tokens), F32)], axis=0).T
-    inverse = jnp.broadcast_to(full[:, 0:1], (tokens, DIM))
-    factor = jnp.broadcast_to(full[:, 1:2], (tokens, DIM))
-
     post, stages, end_state, receive_rest, finish_backward = exchange(
         True, b_send, b_recv, b_tsend, b_trecv, b_pre,
         bs_sem, br_sem, bts_sem, btr_sem, bps_sem, bpr_sem,
     )
-    for r, h in enumerate(other_first):
-        at = spot_columns(h)
-        scaled = gain[:, at] * up[:, at].astype(F32)
-        value = (inverse * scaled - att[:, at] * factor).astype(BF16)
-        grad[:, at] = value
-        post(r, h, dot(wq[at, :], value, (1, 0)))
+    state_sums = [None] * heads
+    for i in range(tiles):
+        rows = slice(i * TILE, (i + 1) * TILE)
+        sums = z_send[i]
+        for number in range(i * (head_n - 1), (i + 1) * (head_n - 1)):
+            z_copies[number].wait_recv()
+            sums = sums + z_recv[number]
+        inverse = lax.rsqrt(sums[0:1] / width + EPSILON)
+        factor = inverse * inverse * inverse * sums[1:2] / width
+        full = jnp.concatenate([inverse, factor, jnp.zeros((DIM - 2, TILE), F32)], axis=0).T
+        inverse = jnp.broadcast_to(full[:, 0:1], (TILE, DIM))
+        factor = jnp.broadcast_to(full[:, 1:2], (TILE, DIM))
+        for r, h in enumerate(other_first):
+            at = spot_columns(h)
+            scaled = gain[:, at] * up[rows, at].astype(F32)
+            value = (inverse * scaled - att[rows, at] * factor).astype(BF16)
+            grad[rows, at] = value
+            added = dot(wq[at, rows], value, (1, 0))
+            state_sums[r] = added if i == 0 else state_sums[r] + added
+            if i == tiles - 1:
+                post(r, h, state_sums[r])
     for copy in z_copies:
         copy.wait_send()
 
@@ -490,6 +516,7 @@
     ctx_n, head_n = lax.axis_size("ctx"), lax.axis_size("head")
     slots = (ctx_n.bit_length() - 2) * heads * PARTS
     half = heads // 2
+    parts = tokens // TILE
     wide = (tokens, local)
     message = (heads, DIM, DIM)
     chip_message = (slots, DIM // PARTS, DIM)
@@ -536,14 +563,14 @@
             pltpu.VMEM((local, tokens), F32),
             *states,
             *states,
-            pltpu.VMEM((2, tokens), F32),
-            pltpu.VMEM((head_n - 1, 2, tokens), F32),
+            pltpu.VMEM((parts, 2, TILE), F32),
+            pltpu.VMEM((parts * (head_n - 1), 2, TILE), F32),
             pltpu.VMEM((ctx_n, 8, DIM), F32),
             dma((6 * COPIES,)),
             *state_sems,
             *state_sems,
-            dma((head_n - 1,)),
-            dma((head_n - 1,)),
+            dma((parts * (head_n - 1),)),
+            dma((parts * (head_n - 1),)),
             dma((ctx_n - 1,)),
             dma((ctx_n - 1,)),
         ],

time: 33.1 us -> 33.2 us (level)
  no operation moved by 1% of the time
where the time goes in v8:
time: 33.2 us; the launch traced here: 32.6 us
  Pallas kernels  31.9 us (96%)
  between operations  0.64 us (2%)
    pallas_call x1, Pallas kernels, on_device(): pl.pallas_call(functools.partial(kernel, ctx_n, head_n, local * head_n),...  30.7 us
    pallas_call x1, Pallas kernels, on_device(): pl.pallas_call(hand_over, out_shape=(out, out, out), in_specs=[in_vmem] *...  1.24 us

profile of v8, /device:TPU:0, one launch (start us, length us, event | category | flops | bytes accessed | tf_op | source)
XLA Modules:
  0.0 32.6 jit_solution(5635056329152491116)
XLA Ops:
  0.6 30.7 %shard_map.85 = (bf16[512,512]{1,0:T(8,128)(2,1)S(1)}, bf16[512,512]{1,0:T(8,128)(2,1)S(1)}, bf16[512,512]{1,0:T(8,128)(2,1)S(1)}) custom-call(bf16[512,512]{1,0:T(8,128)(2,1)} %q_hbm.1, bf16[512,512]{1,0:T(8,128)(2,1)} %k_hbm.1, bf16[512,512]{1,0:T(8,128)(2,1)} %v_hbm.1, f32[4,512]{1,0:T(4,128)} %bitcast.2, f32[1,512]{1,0:T(1,128)} %bitcast.3, ...), custom_call_target="tpu_custom_call" | custom-call | flops 2147483648 | bytes 3670016 | tf_op jit(solution)/shard_map/pallas_call | solution.py:538
  31.4 1.2 %shard_map.86 = (bf16[512,512]{1,0:T(8,128)(2,1)}, bf16[512,512]{1,0:T(8,128)(2,1)}, bf16[512,512]{1,0:T(8,128)(2,1)}) custom-call(bf16[512,512]{1,0:T(8,128)(2,1)S(1)} %get-tuple-element.6.refs_0_, bf16[512,512]{1,0:T(8,128)(2,1)S(1)} %get-tuple-element.7.refs_1_, bf16[512,512]{1,0:T(8,128)(2,1)S(1)} %get-tuple-element.8.refs_2_), custom_call_target="tpu_custom_call" | custom-call | tf_op jit(solution)/shard_map/pallas_call | solution.py:586

commit v9 on v7

--- a/solution.py
+++ b/solution.py
@@ -336,8 +336,8 @@
             total_rows = part if total_rows is None else total_rows + part
         att[rows, columns(h)] = total_rows
 
-    def weigh_queries():
-        for h in range(heads):
+    def weigh_queries(chosen):
+        for h in chosen:
             turned = q[:, columns(h)].T.astype(F32)
             qt[columns(h), :] = turned.astype(BF16)
             wq[columns(h), :] = (turned * jnp.exp(cum_rows[h : h + 1, :])).astype(BF16)
@@ -364,7 +364,9 @@
 
     parts = units(forward)
     middle = len(parts) // 2
-    interleave([[receive_levels], parts[:middle], [spread_factors] + parts[middle:]], stages)
+    early = [functools.partial(weigh_queries, range(half))]
+    late = [functools.partial(weigh_queries, range(half, heads)), spread_factors]
+    interleave([[receive_levels], early + parts[:middle], late + parts[middle:]], stages)
 
     wait(load_gain)
     wait(load_up)
@@ -398,7 +400,6 @@
         )
         copy.start()
         z_copies.append(copy)
-    weigh_queries()
     finish_forward()
     sums = z_send[...]
     for d in range(1, head_n):

time: 33.1 us -> 33.1 us (level)
  no operation moved by 1% of the time
where the time goes in v9:
time: 33.1 us; the launch traced here: 32.5 us
  Pallas kernels  31.8 us (96%)
  between operations  0.64 us (2%)
    pallas_call x1, Pallas kernels, on_device(): pl.pallas_call(functools.partial(kernel, ctx_n, head_n, local * head_n),...  30.6 us
    pallas_call x1, Pallas kernels, on_device(): pl.pallas_call(hand_over, out_shape=(out, out, out), in_specs=[in_vmem] *...  1.24 us

profile of v9, /device:TPU:0, one launch (start us, length us, event | category | flops | bytes accessed | tf_op | source)
XLA Modules:
  0.0 32.5 jit_solution(9801788943476658120)
XLA Ops:
  0.6 30.6 %shard_map.85 = (bf16[512,512]{1,0:T(8,128)(2,1)S(1)}, bf16[512,512]{1,0:T(8,128)(2,1)S(1)}, bf16[512,512]{1,0:T(8,128)(2,1)S(1)}) custom-call(bf16[512,512]{1,0:T(8,128)(2,1)} %q_hbm.1, bf16[512,512]{1,0:T(8,128)(2,1)} %k_hbm.1, bf16[512,512]{1,0:T(8,128)(2,1)} %v_hbm.1, f32[4,512]{1,0:T(4,128)} %bitcast.2, f32[1,512]{1,0:T(1,128)} %bitcast.3, ...), custom_call_target="tpu_custom_call" | custom-call | flops 2147483648 | bytes 3670016 | tf_op jit(solution)/shard_map/pallas_call | solution.py:512
  31.2 1.2 %shard_map.86 = (bf16[512,512]{1,0:T(8,128)(2,1)}, bf16[512,512]{1,0:T(8,128)(2,1)}, bf16[512,512]{1,0:T(8,128)(2,1)}) custom-call(bf16[512,512]{1,0:T(8,128)(2,1)S(1)} %get-tuple-element.6.refs_0_, bf16[512,512]{1,0:T(8,128)(2,1)S(1)} %get-tuple-element.7.refs_1_, bf16[512,512]{1,0:T(8,128)(2,1)S(1)} %get-tuple-element.8.refs_2_), custom_call_target="tpu_custom_call" | custom-call | tf_op jit(solution)/shard_map/pallas_call | solution.py:560
